TPU v7x, 512 devices: a whole 4x4x16 slice. The times are simulated.
512 devices in a mesh: idx: 64 (over x, z), rep: 8 (over y, core).
Axes of the slice: x: 4, y: 4, z: 16, core: 2. Of those that a mesh axis runs over, the one named last changes fastest.
Arguments:
- t_slab: bfloat16 [12800, 51200], P(('idx', 'rep')), may hold values from -6 to 6
- w_cycle: bfloat16 [51200, 400], P(('idx', 'rep')), may hold values from -0.078125 to 0.078125
- a_irrep: int32 [128], replicated, may hold values from 0 to 7
- b_irrep: int32 [4], replicated, may hold values from 0 to 7
- c_irrep: int32 [512], replicated, may hold values from 0 to 7, as said below
- occ_irrep: int32 [100], replicated, may hold values from 0 to 7
- eps_a: float32 [128], replicated, may hold values from 0.5 to 4
- eps_b: float32 [4], replicated, may hold values from 0.5 to 4
- eps_occ: float32 [100], replicated, may hold values from -3 to -0.5
Outputs:
- update: float32 [12800, 400], P(('idx', 'rep'))
Inputs may be any that keep to these rules, and one draw needn't show every extreme that they name: `a_irrep`: D2h irrep labels; the product of two irreps is the bitwise exclusive or of their labels. `b_irrep`: D2h irrep labels. `c_irrep`: D2h irrep labels; each aligned group of 8 consecutive summed virtual orbitals holds each of the 8 irreps exactly once. `occ_irrep`: D2h irrep labels.
All inputs are finite; a program needn't handle non-finite values.
Results may differ from a plain program's by a relative error of at most 0.0003.
Values may be sent and summed in bfloat16 or wider, within the bound.
No kernel may reach another device: no remote copies, remote signals or barrier semaphores. Data moves between devices by JAX's collectives and lax.ppermute only.
A program may use at most 64 MiB of HBM per device.

v0:
```python
import jax
import jax.numpy as jnp
from jax import lax
from jax.sharding import PartitionSpec as P


def lookup(values, where_index):
    positions = jnp.arange(values.shape[0], dtype=jnp.int32)
    picked = jnp.where(
        where_index[:, None] == positions[None, :], values[None, :], jnp.zeros((), values.dtype)
    )
    return jnp.sum(picked, axis=1)


def per_device(t_slab, w_cycle, a_irrep, b_irrep, c_irrep, occ_irrep, eps_a, eps_b, eps_occ):
    idx_count = lax.axis_size("idx")
    rep_count = lax.axis_size("rep")
    idx_place = lax.axis_index("idx")
    rep_place = lax.axis_index("rep")
    occupied = occ_irrep.shape[0]
    rows_dev = t_slab.shape[0]
    columns = t_slab.shape[1] // idx_count
    virt_block = columns // occupied
    slab_width = b_irrep.shape[0]
    local_rows = jnp.arange(idx_count * rows_dev, dtype=jnp.int32)
    global_rows = (
        local_rows // rows_dev * rep_count + rep_place
    ) * rows_dev + local_rows % rows_dev
    row_label = jnp.bitwise_xor(
        lookup(a_irrep, global_rows // occupied), lookup(occ_irrep, global_rows % occupied)
    )
    own_rows = (idx_place * rep_count + rep_place) * rows_dev + jnp.arange(
        rows_dev, dtype=jnp.int32
    )
    own_energy = lookup(eps_a, own_rows // occupied) - lookup(eps_occ, own_rows % occupied)
    all_labels = jnp.bitwise_xor(
        c_irrep.reshape(idx_count, virt_block)[:, :, None], occ_irrep[None, None, :]
    ).reshape(idx_count, columns)
    col_label = lax.dynamic_index_in_dim(all_labels, idx_place, 0, keepdims=False)
    out_label = jnp.bitwise_xor(jnp.repeat(b_irrep, occupied), jnp.tile(occ_irrep, slab_width))
    out_energy = jnp.repeat(eps_b, occupied) - jnp.tile(eps_occ, slab_width)
    zero_amp = jnp.zeros((), jnp.bfloat16)
    gathered = lax.all_gather(w_cycle, "rep", axis=0, tiled=True)
    right = jnp.where(col_label[:, None] == out_label[None, :], gathered, zero_amp)
    exchanged = lax.all_to_all(t_slab, "idx", split_axis=1, concat_axis=0, tiled=True)
    left = jnp.where(row_label[:, None] == col_label[None, :], exchanged, zero_amp)
    cycle = lax.psum_scatter(
        jnp.dot(left, right, preferred_element_type=jnp.float32),
        "idx",
        scatter_dimension=0,
        tiled=True,
    )
    return cycle / (own_energy[:, None] + out_energy[None, :])


def solution(mesh):
    in_specs = (P(("idx", "rep"), None), P(("idx", "rep"), None), P(), P(), P(), P(), P(), P(), P())
    out_specs = P(("idx", "rep"), None)
    return jax.shard_map(
        per_device, mesh=mesh, in_specs=in_specs, out_specs=out_specs, check_vma=False
    )
```

profile of v0, /device:TPU:48, one launch (start us, length us, event | category | flops | bytes accessed | tf_op | source)
XLA Modules:
  0.0 447.4 jit_solution(6919463552579216031)
XLA Ops:
  0.0 6.0 %all_to_all.14 = bf16[25,64,800]{2,1,0:T(8,128)(2,1)S(1)} reshape(bf16[25,51200]{1,0:T(8,128)(2,1)} %param.9) | data formatting | bytes 5120000 | tf_op jit(solution)/shard_map/all_to_all | solution.py:45
  6.0 3.5 copy.14
  9.5 18.5 %all-to-all-start = ((bf16[25,64,800]{2,0,1:T(8,128)(2,1)}), bf16[25,64,800]{2,0,1:T(8,128)(2,1)}, u32[]{:S(2)}, u32[]{:S(2)}) async-start(bf16[25,64,800]{2,0,1:T(8,128)(2,1)} %copy.14), calls=%async_computation | async-start | bytes 7340032 | tf_op jit(solution)/shard_map/all_to_all | solution.py:45
  28.6 12.2 %all-gather = bf16[8,100,400]{1,2,0:T(8,128)(2,1)S(1)} all-gather(bf16[1,100,400]{1,2,0:T(8,128)(2,1)S(1)} %bitcast.7), channel_id=1, replica_groups=mesh['idx'=64,'rep'=8] {'rep'}, dimensions={0}, use_global_device_ids=true | all-gather | bytes 720000 | tf_op jit(solution)/shard_map/all_gather | solution.py:43
  41.0 1.5 reshape.100
  43.5 149.8 %all-to-all-done = bf16[25,64,800]{2,0,1:T(8,128)(2,1)} async-done(((bf16[25,64,800]{2,0,1:T(8,128)(2,1)}), bf16[25,64,800]{2,0,1:T(8,128)(2,1)}, u32[]{:S(2)}, u32[]{:S(2)}) %all-to-all-start) | async-done | bytes 2560032 | tf_op jit(solution)/shard_map/all_to_all | solution.py:45
  193.3 4.9 %all_to_all.17 = bf16[1600,800]{1,0:T(8,128)(2,1)} reshape(bf16[64,25,800]{2,1,0:T(8,128)(2,1)} %bitcast) | data formatting | bytes 5120000 | tf_op jit(solution)/shard_map/all_to_all | solution.py:45
  198.2 4.0 fusion.1
  202.2 169.3 %fusion = f32[32,400]{1,0:T(8,128)S(1)} fusion(f32[1600,400]{1,0:T(8,128)S(1)} %fusion.1), kind=kCustom, calls=%all-reduce-scatter | all-reduce-scatter fusion | flops 819201 | bytes 2613248
  371.6 1.3 collective-permute-start.12
  372.9 1.3 collective-permute-start.11
  374.2 1.3 collective-permute-start.10
  375.5 1.3 collective-permute-start.13
  376.8 19.3 %collective-permute-start.9 = (f32[32,400]{1,0:T(8,128)S(1)}, f32[32,400]{1,0:T(8,128)S(1)}, u32[]{:S(2)}, u32[]{:S(2)}) collective-permute-start(f32[32,400]{1,0:T(8,128)S(1)} %fusion), channel_id=1, source_target_pairs={{0,80},{8,88},{16,96},{24,104},{32,112},{40,120},{48,128},{56,136}... | collective-permute-start | bytes 153608
  396.2 1.6 collective-permute-start.8
  397.8 6.8 %collective-permute-start.7 = (f32[32,400]{1,0:T(8,128)S(1)}, f32[32,400]{1,0:T(8,128)S(1)}, u32[]{:S(2)}, u32[]{:S(2)}) collective-permute-start(f32[32,400]{1,0:T(8,128)S(1)} %fusion), channel_id=1, source_target_pairs={{0,64},{8,72},{16,80},{24,88},{32,96},{40,104},{48,112},{56,120},{... | collective-permute-start | bytes 153608
  404.5 10.7 %collective-permute-start.6 = (f32[32,400]{1,0:T(8,128)S(1)}, f32[32,400]{1,0:T(8,128)S(1)}, u32[]{:S(2)}, u32[]{:S(2)}) collective-permute-start(f32[32,400]{1,0:T(8,128)S(1)} %fusion), channel_id=1, source_target_pairs={{0,56},{8,64},{16,72},{24,80},{32,88},{40,96},{48,104},{56,112},{6... | collective-permute-start | bytes 153608
  416.8 9.2 %collective-permute-start.4 = (f32[32,400]{1,0:T(8,128)S(1)}, f32[32,400]{1,0:T(8,128)S(1)}, u32[]{:S(2)}, u32[]{:S(2)}) collective-permute-start(f32[32,400]{1,0:T(8,128)S(1)} %fusion), channel_id=1, source_target_pairs={{0,40},{8,48},{16,56},{24,64},{32,72},{40,80},{48,88},{56,96},{64,... | collective-permute-start | bytes 153608
  426.0 5.7 %collective-permute-start.3 = (f32[32,400]{1,0:T(8,128)S(1)}, f32[32,400]{1,0:T(8,128)S(1)}, u32[]{:S(2)}, u32[]{:S(2)}) collective-permute-start(f32[32,400]{1,0:T(8,128)S(1)} %fusion), channel_id=1, source_target_pairs={{0,32},{8,40},{16,48},{24,56},{32,64},{40,72},{48,80},{56,88},{64,... | collective-permute-start | bytes 153608
  431.8 3.8 collective-permute-start.2
  435.6 2.9 collective-permute-start.1
  438.5 2.5 collective-permute-start
  443.3 1.4 collective-permute-done
  444.7 2.0 concatenate
  (52 shorter events, 5.4 us)
Async XLA Ops:
  9.5 18.6 %copy-start.2 = (s32[512]{0:T(512)S(1)}, s32[512]{0:T(512)}, u32[]{:S(2)}) copy-start(s32[512]{0:T(512)} %param.13) | copy-start | bytes 6148
  9.5 19.0 %copy-start.1 = (s32[100]{0:T(128)S(1)}, s32[100]{0:T(128)}, u32[]{:S(2)}) copy-start(s32[100]{0:T(128)} %param.14) | copy-start | bytes 1204
  9.5 19.0 %copy-start = (bf16[100,400]{0,1:T(8,128)(2,1)S(1)}, bf16[100,400]{0,1:T(8,128)(2,1)}, u32[]{:S(2)}) copy-start(bf16[100,400]{0,1:T(8,128)(2,1)} %param.10) | copy-start | bytes 240004
  9.5 183.8 %all-to-all-start = ((bf16[25,64,800]{2,0,1:T(8,128)(2,1)}), bf16[25,64,800]{2,0,1:T(8,128)(2,1)}, u32[]{:S(2)}, u32[]{:S(2)}) async-start(bf16[25,64,800]{2,0,1:T(8,128)(2,1)} %copy.14), calls=%async_computation | async-start | bytes 7340032 | tf_op jit(solution)/shard_map/all_to_all | solution.py:45
  28.0 14.5 %copy-start.4 = (s32[4]{0:T(128)S(1)}, s32[4]{0:T(128)}, u32[]{:S(2)}) copy-start(s32[4]{0:T(128)} %param.12) | copy-start | bytes 52
  28.0 14.8 %copy-start.3 = (s32[128]{0:T(128)S(1)}, s32[128]{0:T(128)}, u32[]{:S(2)}) copy-start(s32[128]{0:T(128)} %param.11) | copy-start | bytes 1540
  28.0 15.4 %copy-start.5 = (f32[4]{0:T(128)S(1)}, f32[4]{0:T(128)}, u32[]{:S(2)}) copy-start(f32[4]{0:T(128)} %param.16) | copy-start | bytes 52
  28.1 15.4 %copy-start.6 = (f32[100]{0:T(128)S(1)}, f32[100]{0:T(128)}, u32[]{:S(2)}) copy-start(f32[100]{0:T(128)} %param.17) | copy-start | bytes 1204
  202.2 238.8 %copy-start.7 = (f32[128]{0:T(128)S(1)}, f32[128]{0:T(128)}, u32[]{:S(2)}) copy-start(f32[128]{0:T(128)} %param.15) | copy-start | bytes 1540
  371.6 26.2 %collective-permute-start.12 = (f32[32,400]{1,0:T(8,128)S(1)}, f32[32,400]{1,0:T(8,128)S(1)}, u32[]{:S(2)}, u32[]{:S(2)}) collective-permute-start(f32[32,400]{1,0:T(8,128)S(1)} %fusion), channel_id=1, source_target_pairs={{0,104},{8,112},{16,120},{24,128},{32,136},{40,144},{48,152},{56,1... | collective-permute-start | bytes 153608
  372.9 31.6 %collective-permute-start.11 = (f32[32,400]{1,0:T(8,128)S(1)}, f32[32,400]{1,0:T(8,128)S(1)}, u32[]{:S(2)}, u32[]{:S(2)}) collective-permute-start(f32[32,400]{1,0:T(8,128)S(1)} %fusion), channel_id=1, source_target_pairs={{0,96},{8,104},{16,112},{24,120},{32,128},{40,136},{48,144},{56,15... | collective-permute-start | bytes 153608
  374.2 41.1 %collective-permute-start.10 = (f32[32,400]{1,0:T(8,128)S(1)}, f32[32,400]{1,0:T(8,128)S(1)}, u32[]{:S(2)}, u32[]{:S(2)}) collective-permute-start(f32[32,400]{1,0:T(8,128)S(1)} %fusion), channel_id=1, source_target_pairs={{0,88},{8,96},{16,104},{24,112},{32,120},{40,128},{48,136},{56,144... | collective-permute-start | bytes 153608
  375.5 20.6 %collective-permute-start.13 = (f32[25,400]{1,0:T(8,128)S(1)}, f32[25,400]{1,0:T(8,128)S(1)}, u32[]{:S(2)}, u32[]{:S(2)}) collective-permute-start(f32[25,400]{1,0:T(8,128)S(1)} %slice), channel_id=1, source_target_pairs={{0,112},{8,120},{16,128},{24,136},{32,144},{40,152},{48,160},{56,1... | collective-permute-start | bytes 120008
  376.8 39.9 %collective-permute-start.9 = (f32[32,400]{1,0:T(8,128)S(1)}, f32[32,400]{1,0:T(8,128)S(1)}, u32[]{:S(2)}, u32[]{:S(2)}) collective-permute-start(f32[32,400]{1,0:T(8,128)S(1)} %fusion), channel_id=1, source_target_pairs={{0,80},{8,88},{16,96},{24,104},{32,112},{40,120},{48,128},{56,136}... | collective-permute-start | bytes 153608
  396.2 29.8 %collective-permute-start.8 = (f32[32,400]{1,0:T(8,128)S(1)}, f32[32,400]{1,0:T(8,128)S(1)}, u32[]{:S(2)}, u32[]{:S(2)}) collective-permute-start(f32[32,400]{1,0:T(8,128)S(1)} %fusion), channel_id=1, source_target_pairs={{0,72},{8,80},{16,88},{24,96},{32,104},{40,112},{48,120},{56,128},... | collective-permute-start | bytes 153608
  397.8 34.0 %collective-permute-start.7 = (f32[32,400]{1,0:T(8,128)S(1)}, f32[32,400]{1,0:T(8,128)S(1)}, u32[]{:S(2)}, u32[]{:S(2)}) collective-permute-start(f32[32,400]{1,0:T(8,128)S(1)} %fusion), channel_id=1, source_target_pairs={{0,64},{8,72},{16,80},{24,88},{32,96},{40,104},{48,112},{56,120},{... | collective-permute-start | bytes 153608
  404.5 31.1 %collective-permute-start.6 = (f32[32,400]{1,0:T(8,128)S(1)}, f32[32,400]{1,0:T(8,128)S(1)}, u32[]{:S(2)}, u32[]{:S(2)}) collective-permute-start(f32[32,400]{1,0:T(8,128)S(1)} %fusion), channel_id=1, source_target_pairs={{0,56},{8,64},{16,72},{24,80},{32,88},{40,96},{48,104},{56,112},{6... | collective-permute-start | bytes 153608
  415.3 23.2 %collective-permute-start.5 = (f32[32,400]{1,0:T(8,128)S(1)}, f32[32,400]{1,0:T(8,128)S(1)}, u32[]{:S(2)}, u32[]{:S(2)}) collective-permute-start(f32[32,400]{1,0:T(8,128)S(1)} %fusion), channel_id=1, source_target_pairs={{0,48},{8,56},{16,64},{24,72},{32,80},{40,88},{48,96},{56,104},{64... | collective-permute-start | bytes 153608
  416.8 26.4 %collective-permute-start.4 = (f32[32,400]{1,0:T(8,128)S(1)}, f32[32,400]{1,0:T(8,128)S(1)}, u32[]{:S(2)}, u32[]{:S(2)}) collective-permute-start(f32[32,400]{1,0:T(8,128)S(1)} %fusion), channel_id=1, source_target_pairs={{0,40},{8,48},{16,56},{24,64},{32,72},{40,80},{48,88},{56,96},{64,... | collective-permute-start | bytes 153608
  426.0 17.2 %collective-permute-start.3 = (f32[32,400]{1,0:T(8,128)S(1)}, f32[32,400]{1,0:T(8,128)S(1)}, u32[]{:S(2)}, u32[]{:S(2)}) collective-permute-start(f32[32,400]{1,0:T(8,128)S(1)} %fusion), channel_id=1, source_target_pairs={{0,32},{8,40},{16,48},{24,56},{32,64},{40,72},{48,80},{56,88},{64,... | collective-permute-start | bytes 153608
  431.8 11.5 %collective-permute-start.2 = (f32[32,400]{1,0:T(8,128)S(1)}, f32[32,400]{1,0:T(8,128)S(1)}, u32[]{:S(2)}, u32[]{:S(2)}) collective-permute-start(f32[32,400]{1,0:T(8,128)S(1)} %fusion), channel_id=1, source_target_pairs={{0,24},{8,32},{16,40},{24,48},{32,56},{40,64},{48,72},{56,80},{64,... | collective-permute-start | bytes 153608
  435.6 7.6 %collective-permute-start.1 = (f32[32,400]{1,0:T(8,128)S(1)}, f32[32,400]{1,0:T(8,128)S(1)}, u32[]{:S(2)}, u32[]{:S(2)}) collective-permute-start(f32[32,400]{1,0:T(8,128)S(1)} %fusion), channel_id=1, source_target_pairs={{0,16},{8,24},{16,32},{24,40},{32,48},{40,56},{48,64},{56,72},{64,... | collective-permute-start | bytes 153608
  438.5 6.2 %collective-permute-start = (f32[32,400]{1,0:T(8,128)S(1)}, f32[32,400]{1,0:T(8,128)S(1)}, u32[]{:S(2)}, u32[]{:S(2)}) collective-permute-start(f32[32,400]{1,0:T(8,128)S(1)} %fusion), channel_id=1, source_target_pairs={{0,8},{8,16},{16,24},{24,32},{32,40},{40,48},{48,56},{56,64},{64,7... | collective-permute-start | bytes 153608
where the time goes:
time: 448 us; the launch traced here: 447 us
  blocking collectives  182 us (41%)
  waiting for transfers between devices  151 us (34%)
  starting transfers between devices  87.5 us (20%)
  local copies, waits for them, and re-layouts  20 us (4%)
    unnamed x1, blocking collectives  169 us
    all_to_all x1, waiting for transfers between devices, per_device(): lax.all_to_all(t_slab, 'idx', split_axis=1, concat_axis=0, tiled=True)  150 us
    unnamed x14, starting transfers between devices  69 us
    all_to_all x1, starting transfers between devices, per_device(): lax.all_to_all(t_slab, 'idx', split_axis=1, concat_axis=0, tiled=True)  18.5 us
    all_to_all x3, local copies, waits for them, and re-layouts, per_device(): lax.all_to_all(t_slab, 'idx', split_axis=1, concat_axis=0, tiled=True)  14.4 us
    all_gather x1, blocking collectives, per_device(): gathered = lax.all_gather(w_cycle, 'rep', axis=0, tiled=True)  12.2 us
  transfers between devices with their start and end apart: 15, of which 2 were waited for; matrix products, arithmetic and copies ran while one was open for 1% of the time, Pallas kernels for 0%

commit v1 on v0

v1 whole, which is shorter than its diff:
```python
import jax
import jax.numpy as jnp
import numpy as np
from jax import lax
from jax.experimental import pallas as pl
from jax.experimental.pallas import tpu as pltpu
from jax.sharding import PartitionSpec as P

O = 100
G = 8
KP = 32
NP = 256
RP = 32
ROWS = 25
CHUNK = 4 * G * O
F32, BF16, I32 = jnp.float32, jnp.bfloat16, jnp.int32
VMEM = pl.BlockSpec(memory_space=pltpu.VMEM)
SMEM = pl.BlockSpec(memory_space=pltpu.SMEM)
ZS, XS, YS, CS = 16, 4, 4, 2
Z_GROUPS = [[x * ZS + z for z in range(ZS)] for x in range(XS)]
X_GROUPS = [[x * ZS + z for x in range(XS)] for z in range(ZS)]


def iota(shape, dim):
    return lax.broadcasted_iota(I32, shape, dim)


def to_rows(lanes, count, first):
    shape = (count, lanes.shape[1])
    hit = iota(shape, 1) == iota(shape, 0) + first
    return jnp.sum(jnp.where(hit, lanes, 0.0), axis=1, keepdims=True)


def tiled(lanes, width):
    rows = to_rows(lanes, 104, 0)
    shape = (104, width)
    s = iota(shape, 1)
    mod = s - O * ((s >= O).astype(I32) + (s >= 2 * O).astype(I32) + (s >= 3 * O).astype(I32))
    return jnp.sum(jnp.where(iota(shape, 0) == mod, rows, 0.0), axis=0, keepdims=True)


def by_slab(ref, width, dtype):
    s = iota((1, width), 1)
    out = jnp.full((1, width), ref[0], dtype)
    for b in range(1, 4):
        out = jnp.where(s >= b * O, ref[b], out)
    return out


def w_kernel(place, c_irrep, b_irrep, occ, w_ref, out_ref):
    occ_f = occ[...].astype(F32)
    row = c_irrep[place[0]] ^ to_rows(occ_f, 100, 0).astype(I32)
    col = by_slab(b_irrep, 400, I32) ^ tiled(occ_f, 400).astype(I32)
    kept = jnp.where(row == col, w_ref[...].astype(F32), 0.0)
    full = jnp.concatenate([kept, jnp.zeros((28, 400), F32)], axis=0)
    for y in range(YS):
        part = full[KP * y : KP * y + KP].astype(BF16)
        out_ref[CS * y] = part[:, :NP]
        out_ref[CS * y + 1, :, : 400 - NP] = part[:, NP:]
        out_ref[CS * y + 1, :, 400 - NP :] = jnp.zeros((KP, 2 * NP - 400), BF16)


def t_kernel(place, a_irrep, occ, c_rows, spread, tile, pick, t_ref, out_ref, want, have, kept):
    step = pl.program_id(0)

    @pl.when(step == 0)
    def _():
        occ_f = occ[...].astype(F32)
        row = a_irrep[place[0] // 4] ^ to_rows(occ_f, RP, ROWS * (place[0] % 4)).astype(I32)
        occ_t = jnp.dot(
            jnp.broadcast_to(occ_f, (8, O)).astype(BF16), tile[...], preferred_element_type=F32
        )
        want[...] = (row ^ occ_t[:1].astype(I32)).astype(BF16)
        have[...] = jnp.dot(
            c_rows[...].astype(F32).astype(BF16), spread[...], preferred_element_type=F32
        )
        kept[...] = jnp.zeros_like(kept)

    for h in range(2):
        label = have[pl.ds(2 * step + h, 1), :].astype(BF16)
        mask = want[:ROWS, :] == label
        block = t_ref[:, CHUNK * h : CHUNK * (h + 1)]
        kept[RP * h : RP * h + ROWS, :] = jnp.where(mask, block, jnp.zeros((), BF16))
    packed = jnp.dot(kept[...], pick[...], preferred_element_type=F32).astype(BF16)
    for h in range(2):
        for y in range(YS):
            part = packed[RP * h : RP * h + RP, 128 * y : 128 * y + 128]
            for c in range(CS):
                out_ref[CS * y + c, :, pl.ds(pl.multiple_of(256 * step + 128 * h, 128), 128)] = part


def mm_kernel(t_ref, w_ref, out_ref):
    out_ref[...] = jnp.dot(t_ref[...], w_ref[...], preferred_element_type=F32)


def end_kernel(place, a_irrep, b_irrep, eps_a, eps_b, occ, eps_occ, part_ref, out_ref):
    first = ROWS * (place[0] % 4)
    a = place[0] // 4
    occ_f = occ[...].astype(F32)
    eo = eps_occ[...]
    row = a_irrep[a] ^ to_rows(occ_f, ROWS, first).astype(I32)
    col = by_slab(b_irrep, 400, I32) ^ tiled(occ_f, 400).astype(I32)
    energy = (eps_a[a] - to_rows(eo, ROWS, first)) + (by_slab(eps_b, 400, F32) - tiled(eo, 400))
    for c, lo, hi in ((0, 0, NP), (1, NP, 400)):
        total = part_ref[c, :ROWS, : hi - lo]
        for y in range(1, YS):
            total = total + part_ref[CS * y + c, :ROWS, : hi - lo]
        total = jnp.where(row == col[:, lo:hi], total, 0.0)
        out_ref[:, lo:hi] = total / energy[:, lo:hi]


def tables():
    lane = np.arange(CHUNK)
    j, k = lane // (G * O), lane % O
    spread = (np.arange(32)[:, None] == lane[None, :] // O).astype(jnp.bfloat16)
    tile = (np.arange(O)[:, None] == k[None, :]).astype(jnp.bfloat16)
    target = (k // KP) * 128 + j * KP + k % KP
    pick = (target[:, None] == np.arange(512)[None, :]).astype(jnp.bfloat16)
    return spread, tile, pick


def call(kernel, shape, dtype, specs, flops, moved, **rest):
    return pl.pallas_call(
        kernel,
        out_shape=jax.ShapeDtypeStruct(shape, dtype),
        in_specs=specs,
        cost_estimate=pl.CostEstimate(flops=flops, bytes_accessed=moved, transcendentals=0),
        compiler_params=pltpu.CompilerParams(vmem_limit_bytes=40 * 2**20),
        **rest,
    )


def per_device(t_slab, w_cycle, a_irrep, b_irrep, c_irrep, occ_irrep, eps_a, eps_b, eps_occ):
    place = (lax.axis_index("idx") * (YS * CS) + lax.axis_index("rep")).astype(I32).reshape(1)
    occ = occ_irrep.reshape(1, O)
    spread, tile, pick = (jnp.asarray(table) for table in tables())
    w_parts = call(
        w_kernel, (8, KP, NP), BF16, [SMEM, SMEM, SMEM, VMEM, VMEM], 10**6, 2 * 10**5,
        out_specs=VMEM,
    )(place, c_irrep, b_irrep, occ, w_cycle)
    w_got = lax.all_to_all(w_parts, "rep", split_axis=0, concat_axis=0, tiled=True)
    w_own = jnp.sum(w_got, axis=0, dtype=BF16)

    const = lambda *shape: pl.BlockSpec(shape, lambda i: (0,) * len(shape))
    t_parts = call(
        t_kernel, (8, RP, 64 * KP), BF16,
        [SMEM, SMEM, const(1, O), const(16, 32), const(32, CHUNK), const(O, CHUNK), const(CHUNK, 512),
         pl.BlockSpec((ROWS, 2 * CHUNK), lambda i: (0, i))],
        2 * 512 * CHUNK * 512, 8 * 10**6,
        grid=(8,),
        out_specs=const(8, RP, 64 * KP),
        scratch_shapes=[
            pltpu.VMEM((RP, CHUNK), BF16),
            pltpu.VMEM((16, CHUNK), F32),
            pltpu.VMEM((2 * RP, CHUNK), BF16),
        ],
    )(place, a_irrep, occ, c_irrep.reshape(16, 32), spread, tile, pick, t_slab)
    t_got = lax.all_to_all(t_parts, "rep", split_axis=0, concat_axis=0, tiled=True)

    w_z = lax.all_to_all(
        jnp.broadcast_to(w_own[None], (ZS, KP, NP)), "idx", split_axis=0, concat_axis=0,
        axis_index_groups=Z_GROUPS, tiled=True,
    )
    w_all = lax.all_gather(w_z, "idx", axis=0, axis_index_groups=X_GROUPS)
    partial = call(
        mm_kernel, (8 * RP, NP), F32, [VMEM, VMEM], 2 * 256 * 2048 * 256, 2 * 10**6, out_specs=VMEM
    )(t_got.reshape(8 * RP, 64 * KP), w_all.reshape(64 * KP, NP))
    ends = lax.all_to_all(partial.reshape(8, RP, NP), "rep", split_axis=0, concat_axis=0, tiled=True)
    return call(
        end_kernel, (ROWS, 400), F32, [SMEM, SMEM, SMEM, SMEM, SMEM, VMEM, VMEM, VMEM], 10**6, 3 * 10**5,
        out_specs=VMEM,
    )(place, a_irrep, b_irrep, eps_a, eps_b, occ, eps_occ.reshape(1, O), ends)


def solution(mesh):
    in_specs = (P(("idx", "rep"), None), P(("idx", "rep"), None), P(), P(), P(), P(), P(), P(), P())
    out_specs = P(("idx", "rep"), None)
    return jax.shard_map(
        per_device, mesh=mesh, in_specs=in_specs, out_specs=out_specs, check_vma=False
    )
```

time: 448 us -> 109 us (0.24)
  the two profiles are of different devices: /device:TPU:48 before, /device:TPU:1 now
where the time goes in v1:
time: 109 us; the launch traced here: 108 us
  blocking collectives  72.9 us (67%)
  between operations  13.5 us (12%)
  local copies, waits for them, and re-layouts  12.2 us (11%)
  Pallas kernels  9.29 us (9%)
    all_to_all x1, blocking collectives, per_device(): lax.all_to_all(jnp.broadcast_to(w_own[None], (ZS, KP, NP)), 'idx', split_...  24.3 us
    all_to_all x1, blocking collectives, per_device(): lax.all_to_all(t_parts, 'rep', split_axis=0, concat_axis=0, tiled=True)  24.1 us
    all_to_all x1, blocking collectives, per_device(): lax.all_to_all(w_parts, 'rep', split_axis=0, concat_axis=0, tiled=True)  14.5 us
    unnamed x33, local copies, waits for them, and re-layouts  11.5 us
    all_to_all x1, blocking collectives, per_device(): lax.all_to_all(partial.reshape(8, RP, NP), 'rep', split_axis=0, concat_ax...  9.94 us
    pallas_call x1, Pallas kernels, per_device(): call(t_kernel, (8, RP, 64 * KP), BF16, [SMEM, SMEM, const(1, O), const(16...  6.82 us
  transfers between devices with their start and end apart: 1, of which 0 were waited for; matrix products, arithmetic and copies ran while one was open for 1% of the time, Pallas kernels for 6%

profile of v1, /device:TPU:1, one launch (start us, length us, event | category | flops | bytes accessed | tf_op | source)
XLA Modules:
  0.0 108.0 jit_solution(6329199859729134690)
XLA Ops:
  6.5 1.0 copy.14.w_ref
  7.6 0.7 copy-done.5
  8.2 0.7 copy-done.6
  8.9 0.7 copy-done.11
  9.6 0.7 shard_map.119
  10.3 14.5 %all_to_all.20 = bf16[8,32,256]{2,1,0:T(8,128)(2,1)S(1)} all-to-all(bf16[8,32,256]{2,1,0:T(8,128)(2,1)S(1)} %shard_map.119), channel_id=1, replica_groups=mesh['idx'=64,'rep'=8] {'rep'}, dimensions={0} | all-to-all | bytes 262144 | tf_op jit(solution)/shard_map/all_to_all | solution.py:141
  24.8 24.3 %all_to_all.21 = bf16[16,32,256]{2,1,0:T(8,128)(2,1)} all-to-all(bf16[16,32,256]{2,1,0:T(8,128)(2,1)S(1)} %broadcast_in_dim.2), channel_id=1, replica_groups={{0,8,16,24,32,40,48,56,64,72,80,88,96,104,112,120},{128,136,144,152,160..., dimensions={0} | all-to-all | bytes 524288 | tf_op jit(solution)/shard_map/all_to_all | solution.py:160
  49.2 0.0 all-gather.3.cloned.1.call-update
  49.2 0.8 reshape.25.c_rows
  50.0 1.9 %copy-done = bf16[25,51200]{1,0:T(8,128)(2,1)S(1)} copy-done((bf16[25,51200]{1,0:T(8,128)(2,1)S(1)}, bf16[25,51200]{1,0:T(8,128)(2,1)}, u32[]{:S(2)}) %copy-start) | copy-done | bytes 2560024
  51.9 1.9 %copy-done.1 = bf16[3200,512]{1,0:T(8,128)(2,1)S(1)} copy-done((bf16[3200,512]{1,0:T(8,128)(2,1)S(1)}, bf16[3200,512]{1,0:T(8,128)(2,1)}, u32[]{:S(2)}) %copy-start.1) | copy-done | bytes 3276824
  53.8 1.1 %copy-done.3 = bf16[100,3200]{1,0:T(8,128)(2,1)S(1)} copy-done((bf16[100,3200]{1,0:T(8,128)(2,1)S(1)}, bf16[100,3200]{1,0:T(8,128)(2,1)}, u32[]{:S(2)}) %copy-start.3) | copy-done | bytes 640024
  54.9 0.9 copy-done.4
  55.8 0.7 copy-done.7
  56.5 0.7 copy-done.9
  57.1 6.8 %shard_map.118 = bf16[8,32,2048]{2,1,0:T(8,128)(2,1)S(1)} custom-call(s32[1]{0:T(128)} %bitcast.place, s32[128]{0:T(128)S(1)} %copy-done.9, s32[1,100]{1,0:T(1,128)S(1)} %bitcast.10, s32[16,32]{1,0:T(8,128)S(1)} %reshape.25.c_rows, bf16[32,3200]{1,0:T(8,128)(2,1)S(1)} %copy-done.4, bf16[100,3200]{1,0:T(8,128)(2,1)S(1)} %copy-done.3, ...), custom_call_target="tpu_custom_call" | custom-call | flops 1677721600 | bytes 8000000 | tf_op jit(solution)/shard_map/pallas_call | solution.py:145
  64.0 0.0 copy-start.10
  64.0 0.0 copy-start.12
  64.0 0.0 copy-start.15
  64.0 24.1 %all_to_all.22 = bf16[8,32,2048]{2,1,0:T(8,128)(2,1)S(1)} all-to-all(bf16[8,32,2048]{2,1,0:T(8,128)(2,1)S(1)} %shard_map.118), channel_id=1, replica_groups=mesh['idx'=64,'rep'=8] {'rep'}, dimensions={0} | all-to-all | bytes 2097152 | tf_op jit(solution)/shard_map/all_to_all | solution.py:158
  88.2 1.2 %copy-done.2 = bf16[64,32,256]{2,1,0:T(8,128)(2,1)S(1)} copy-done((bf16[64,32,256]{2,1,0:T(8,128)(2,1)S(1)}, bf16[64,32,256]{2,1,0:T(8,128)(2,1)}, u32[]{:S(2)}) %copy-start.2) | copy-done | bytes 1048600
  89.4 0.4 shard_map.120
  89.8 9.9 %all_to_all.23.part_ref = f32[8,32,256]{2,1,0:T(8,128)S(1)} all-to-all(f32[8,32,256]{2,1,0:T(8,128)S(1)} %bitcast.7), channel_id=1, replica_groups=mesh['idx'=64,'rep'=8] {'rep'}, dimensions={0} | all-to-all | bytes 524288 | tf_op jit(solution)/shard_map/all_to_all | solution.py:168
  99.8 1.3 %shard_map.121 = f32[25,400]{1,0:T(8,128)} custom-call(s32[1]{0:T(128)} %bitcast.place, s32[128]{0:T(128)S(1)} %copy-done.10, s32[4]{0:T(128)S(1)} %copy-done.12, f32[128]{0:T(128)S(1)} %copy-done.13, f32[4]{0:T(128)S(1)} %copy-done.14, s32[1,100]{1,0:T(1,128)S(1)} %bitcast.11, f32[1,100]{1,0:T(1,128)S(1)} %bitcast.12, f32[8,32,256]{2,1,0:T(8,128)S(1)} %all_to_all.23.part_ref), custom_call_target="tpu_custom_call" | custom-call | flops 1000000 | bytes 300000 | tf_op jit(solution)/shard_map/pallas_call | solution.py:169
  (23 shorter events, 0.1 us)
Async XLA Ops:
  6.5 81.6 %all-gather.3.cloned.1.call-start = ((), (), s32[]{:S(2)}) async-start(), calls=%async_computation.4 | async-start | bytes 1310720 | tf_op jit(solution)/shard_map/all_gather | solution.py:164
  7.6 0.7 copy-start.5
  8.2 0.7 copy-start.6
  8.9 0.7 copy-start.11
  50.0 1.9 %copy-start = (bf16[25,51200]{1,0:T(8,128)(2,1)S(1)}, bf16[25,51200]{1,0:T(8,128)(2,1)}, u32[]{:S(2)}) copy-start(bf16[25,51200]{1,0:T(8,128)(2,1)} %t_ref.1) | copy-start | bytes 7680004
  51.9 1.9 %copy-start.1 = (bf16[3200,512]{1,0:T(8,128)(2,1)S(1)}, bf16[3200,512]{1,0:T(8,128)(2,1)}, u32[]{:S(2)}) copy-start(bf16[3200,512]{1,0:T(8,128)(2,1)} %constant.21.clone.pick) | copy-start | bytes 9830404
  53.8 1.1 %copy-start.3 = (bf16[100,3200]{1,0:T(8,128)(2,1)S(1)}, bf16[100,3200]{1,0:T(8,128)(2,1)}, u32[]{:S(2)}) copy-start(bf16[100,3200]{1,0:T(8,128)(2,1)} %constant.20.clone.tile) | copy-start | bytes 1920004
  54.9 0.9 copy-start.4
  55.8 0.7 copy-start.7
  56.5 0.7 copy-start.9
  64.0 35.8 %copy-start.8 = (s32[100]{0:T(128)S(1)}, s32[100]{0:T(128)}, u32[]{:S(2)}) copy-start(s32[100]{0:T(128)} %param.17) | copy-start | bytes 1204
  64.0 35.8 %copy-start.10 = (s32[128]{0:T(128)S(1)}, s32[128]{0:T(128)}, u32[]{:S(2)}) copy-start(s32[128]{0:T(128)} %a_irrep.3) | copy-start | bytes 1540
  64.0 35.8 %copy-start.12 = (s32[4]{0:T(128)S(1)}, s32[4]{0:T(128)}, u32[]{:S(2)}) copy-start(s32[4]{0:T(128)} %b_irrep.3) | copy-start | bytes 52
  64.0 35.8 %copy-start.13 = (f32[128]{0:T(128)S(1)}, f32[128]{0:T(128)}, u32[]{:S(2)}) copy-start(f32[128]{0:T(128)} %eps_a.1) | copy-start | bytes 1540
  64.0 35.8 %copy-start.14 = (f32[4]{0:T(128)S(1)}, f32[4]{0:T(128)}, u32[]{:S(2)}) copy-start(f32[4]{0:T(128)} %eps_b.1) | copy-start | bytes 52
  64.0 35.8 %copy-start.15 = (f32[100]{0:T(128)S(1)}, f32[100]{0:T(128)}, u32[]{:S(2)}) copy-start(f32[100]{0:T(128)} %param.20) | copy-start | bytes 1204
  88.2 1.2 %copy-start.2 = (bf16[64,32,256]{2,1,0:T(8,128)(2,1)S(1)}, bf16[64,32,256]{2,1,0:T(8,128)(2,1)}, u32[]{:S(2)}) copy-start(bf16[64,32,256]{2,1,0:T(8,128)(2,1)} %all-gather.3.cloned.1.call-done) | copy-start | bytes 3145732
Sparse Core Ops, SparseCore 0:
  49.3 29.3 all-gather.2

commit v2 on v0

v2 whole, which is shorter than its diff:
```python
import jax
import jax.numpy as jnp
from jax import lax
from jax.experimental import pallas as pl
from jax.experimental.pallas import tpu as pltpu
from jax.sharding import PartitionSpec as P

O = 100
G = 8
COLS = 400
KP = 64
NP = 128
RP = 32
ROWS = 25
GROUP = G * O
CHUNK = 4 * GROUP
CHUNKS = 16
STEP = 4
WINDOW = 896
F32, BF16, I32 = jnp.float32, jnp.bfloat16, jnp.int32
HBM = pl.BlockSpec(memory_space=pltpu.HBM)
ZS, XS, YS, CS = 16, 4, 4, 2
Z_GROUPS = [[x * ZS + z for z in range(ZS)] for x in range(XS)]
PLANES = [
    [(x * ZS + z) * YS * CS + p for x in range(XS) for p in range(YS * CS)] for z in range(ZS)
]


def iota(shape, dim):
    return lax.broadcasted_iota(I32, shape, dim)


def mod_o(n):
    return n - O * jnp.floor((n.astype(F32) + 0.5) * (1.0 / O)).astype(I32)


def to_rows(lanes, count, first):
    shape = (count, lanes.shape[1])
    hit = iota(shape, 1) == iota(shape, 0) + first
    return jnp.sum(jnp.where(hit, lanes, 0.0), axis=1, keepdims=True)


def tiled(lanes, width):
    rows = to_rows(lanes, 104, 0)
    hit = iota((104, width), 0) == mod_o(iota((1, width), 1))
    return jnp.sum(jnp.where(hit, rows, 0.0), axis=0, keepdims=True)


def by_slab(ref, dtype):
    s = iota((1, COLS), 1)
    out = jnp.full((1, COLS), ref[0], dtype)
    for b in range(1, COLS // O):
        out = jnp.where(s >= b * O, ref[b], out)
    return out


def place():
    return lax.axis_index("idx") * (YS * CS) + lax.axis_index("rep")


def fetch(sources, targets, sems):
    copies = [pltpu.make_async_copy(s, t, sems.at[i]) for i, (s, t) in enumerate(zip(sources, targets))]
    for copy in copies:
        copy.start()
    for copy in copies:
        copy.wait()


def w_kernel(c_hbm, b_hbm, occ_hbm, w_hbm, out_ref, c_irrep, b_irrep, occ, w_ref, flat, sems):
    fetch((c_hbm, b_hbm, occ_hbm, w_hbm), (c_irrep, b_irrep, occ, w_ref), sems)
    occ_f = occ[...].astype(F32)
    s = iota((COLS, 1), 0)
    slab = jnp.full((COLS, 1), b_irrep[0], I32)
    for b in range(1, COLS // O):
        slab = jnp.where(s >= b * O, b_irrep[b], slab)
    hit = iota((COLS, O), 1) == mod_o(s)
    col = slab ^ jnp.sum(jnp.where(hit, occ_f, 0.0), axis=1, keepdims=True).astype(I32)
    row = c_irrep[place()] ^ occ[...]
    flat[...] = jnp.zeros_like(flat)
    flat[:COLS, :O] = jnp.where(row == col, w_ref[...].astype(F32), 0.0)
    for n in range(4):
        part = flat[NP * n : NP * n + NP, :].T.astype(BF16)
        for half in range(2):
            out_ref[4 * half + n] = part[KP * half : KP * half + KP]


def t_kernel(
    a_hbm, c_hbm, occ_hbm, t_hbm, out_ref, a_irrep, c_lanes, occ, t_ref, want, have, pick, kept, sems, t_sems
):
    def block(q):
        lanes = pl.ds(CHUNK * q, CHUNK)
        return pltpu.make_async_copy(t_hbm.at[:, lanes], t_ref.at[:, lanes], t_sems.at[q])

    small = [
        pltpu.make_async_copy(s, t, sems.at[i])
        for i, (s, t) in enumerate(((a_hbm, a_irrep), (c_hbm, c_lanes), (occ_hbm, occ)))
    ]
    for copy in small:
        copy.start()
    for q in range(CHUNKS):
        block(q).start()
    for j in range(4):
        at = iota((WINDOW, 1), 0) - 32 * j
        k = jnp.where((at >= 0) & (at < GROUP), mod_o(jnp.maximum(at, 0)), -1)
        pick[j] = jnp.where(k == iota((WINDOW, 128), 1), 1.0, 0.0).astype(BF16)
    fold = jnp.where(iota((512, 128), 0) % 32 == iota((512, 128), 1), 1.0, 0.0).astype(BF16)
    lane = iota((128, CHUNK), 1)
    first = O * iota((128, 1), 0)
    spread = jnp.where((lane >= first) & (lane < first + O), 1.0, 0.0).astype(BF16)
    for q in range(CHUNKS):
        kept[RP * q + 16 : RP * q + RP, :] = jnp.zeros((16, CHUNK), BF16)
    for copy in small:
        copy.wait()
    here = place()
    occ_f = occ[...].astype(F32)
    row = a_irrep[here // 4] ^ to_rows(occ_f, RP, ROWS * (here % 4)).astype(I32)
    want[...] = (row ^ tiled(occ_f, CHUNK).astype(I32)).astype(BF16)
    shape = (CHUNKS, 512)
    mine = jnp.where(iota(shape, 1) // 32 == iota(shape, 0), c_lanes[...].astype(F32), 0.0)
    rows = jnp.dot(mine.astype(BF16), fold, preferred_element_type=F32).astype(BF16)
    have[...] = jnp.dot(rows, spread, preferred_element_type=F32)
    for q in range(CHUNKS):
        block(q).wait()
        mask = want[:ROWS, :] == have[q : q + 1, :].astype(BF16)
        got = t_ref[:, CHUNK * q : CHUNK * (q + 1)]
        kept[RP * q : RP * q + ROWS, :] = jnp.where(mask, got, jnp.zeros((), BF16))
    low = iota((CHUNKS * RP, 128), 1) < KP
    for pair in range(2):
        even, odd = (
            jnp.dot(kept[:, 768 * j : 768 * j + WINDOW], pick[j], preferred_element_type=F32)
            for j in (2 * pair, 2 * pair + 1)
        )
        halves = (
            jnp.where(low, even, pltpu.roll(odd, KP, 1)),
            jnp.where(low, pltpu.roll(even, KP, 1), odd),
        )
        for half in range(2):
            packed = halves[half].astype(BF16)
            for q in range(CHUNKS):
                x, h = divmod(q, CHUNKS // XS)
                lanes = slice(256 * h + 128 * pair, 256 * h + 128 * pair + 128)
                part = packed[RP * q : RP * q + RP]
                for n in range(4):
                    out_ref[YS * CS * x + 4 * half + n, :, lanes] = part


def mm_kernel(
    t_ref, w_ref, a_hbm, b_hbm, ea_hbm, eb_hbm, occ_hbm, eo_hbm, out_ref, energy_ref, same_ref,
    a_irrep, b_irrep, eps_a, eps_b, occ, eps_occ, sems
):
    copies = [
        pltpu.make_async_copy(s, t, sems.at[i])
        for i, (s, t) in enumerate(
            zip((a_hbm, b_hbm, ea_hbm, eb_hbm, occ_hbm, eo_hbm), (a_irrep, b_irrep, eps_a, eps_b, occ, eps_occ))
        )
    ]
    for copy in copies:
        copy.start()
    out_ref[...] = jnp.dot(t_ref[...], w_ref[...], preferred_element_type=F32)
    for copy in copies:
        copy.wait()
    here = place()
    first = ROWS * (here % 4)
    a = here // 4
    occ_f, eo = occ[...].astype(F32), eps_occ[...]
    row = a_irrep[a] ^ to_rows(occ_f, ROWS, first).astype(I32)
    col = by_slab(b_irrep, I32) ^ tiled(occ_f, COLS).astype(I32)
    energy_ref[...] = (eps_a[a] - to_rows(eo, ROWS, first)) + (by_slab(eps_b, F32) - tiled(eo, COLS))
    same_ref[...] = jnp.where(row == col, 1.0, 0.0)


def end_kernel(energy_ref, same_ref, part_ref, out_ref):
    for n in range(4):
        lo, hi = NP * n, min(NP * n + NP, COLS)
        total = None
        for x in range(XS):
            for half in range(2):
                part = part_ref[YS * CS * x + 4 * half + n, :ROWS, : hi - lo]
                total = part if total is None else total + part
        total = jnp.where(same_ref[:, lo:hi] > 0.5, total, 0.0)
        out_ref[:, lo:hi] = total / energy_ref[:, lo:hi]


def call(kernel, shape, dtype, flops, moved, room=48, **rest):
    return pl.pallas_call(
        kernel,
        out_shape=(
            [jax.ShapeDtypeStruct(one, dtype) for one in shape]
            if isinstance(shape, list)
            else jax.ShapeDtypeStruct(shape, dtype)
        ),
        cost_estimate=pl.CostEstimate(flops=flops, bytes_accessed=moved, transcendentals=0),
        compiler_params=pltpu.CompilerParams(vmem_limit_bytes=room * 2**20),
        **rest,
    )


def per_device(t_slab, w_cycle, a_irrep, b_irrep, c_irrep, occ_irrep, eps_a, eps_b, eps_occ):
    vmem, smem, dma = pltpu.VMEM, pltpu.SMEM, pltpu.SemaphoreType.DMA
    whole = pl.BlockSpec(memory_space=pltpu.VMEM)
    occ, eo = occ_irrep.reshape(1, O), eps_occ.reshape(1, O)
    w_parts = call(
        w_kernel, (8, KP, NP), BF16, 10**6, 2 * 10**5, room=58,
        in_specs=[HBM] * 4,
        out_specs=whole,
        scratch_shapes=[
            smem((512,), I32), smem((4,), I32), vmem((1, O), I32), vmem((COLS, O), BF16),
            vmem((4 * NP, 2 * KP), F32), dma((4,)),
        ],
    )(c_irrep, b_irrep, occ, w_cycle.T)
    occ_late, w_parts = lax.optimization_barrier((occ, w_parts))
    w_got = lax.all_to_all(w_parts, "rep", split_axis=0, concat_axis=0, tiled=True)
    w_own = jnp.sum(w_got, axis=0, dtype=BF16)
    t_parts = call(
        t_kernel, (XS * YS * CS, RP, 16 * KP), BF16, 4 * 10**9, 4 * 10**6, room=58,
        in_specs=[HBM] * 4,
        out_specs=whole,
        scratch_shapes=[
            smem((128,), I32),
            vmem((1, 512), I32),
            vmem((1, O), I32),
            vmem((ROWS, CHUNKS * CHUNK), BF16),
            vmem((RP, CHUNK), BF16),
            vmem((CHUNKS, CHUNK), F32),
            vmem((4, WINDOW, 128), BF16),
            vmem((CHUNKS * RP, CHUNK), BF16),
            dma((3,)),
            dma((CHUNKS,)),
        ],
    )(a_irrep, c_irrep.reshape(1, 512), occ_late, t_slab)
    t_got = lax.all_to_all(
        t_parts, ("idx", "rep"), split_axis=0, concat_axis=0, axis_index_groups=PLANES, tiled=True
    )

    w_own, t_parts = lax.optimization_barrier((w_own, t_parts))
    w_z = lax.all_gather(w_own, "idx", axis=0, axis_index_groups=Z_GROUPS)
    partial, energy, same = call(
        mm_kernel, [(XS * YS * CS * RP, NP), (ROWS, COLS), (ROWS, COLS)], F32, 2 * 1024 * 1024 * 128, 3 * 10**6, room=24,
        in_specs=[whole] * 2 + [HBM] * 6,
        out_specs=[whole] * 3,
        scratch_shapes=[
            smem((128,), I32), smem((4,), I32), smem((128,), F32), smem((4,), F32),
            vmem((1, O), I32), vmem((1, O), F32), dma((6,)),
        ],
    )(t_got.reshape(-1, 16 * KP), w_z.reshape(ZS * KP, NP), a_irrep, b_irrep, eps_a, eps_b, occ, eo)
    ends = lax.all_to_all(
        partial.reshape(-1, RP, NP), ("idx", "rep"), split_axis=0, concat_axis=0,
        axis_index_groups=PLANES, tiled=True,
    )
    return call(
        end_kernel, (ROWS, COLS), F32, 10**6, 10**6, room=24, in_specs=[whole] * 3, out_specs=whole
    )(energy, same, ends)


def solution(mesh):
    in_specs = (P(("idx", "rep"), None), P(("idx", "rep"), None), P(), P(), P(), P(), P(), P(), P())
    out_specs = P(("idx", "rep"), None)
    return jax.shard_map(
        per_device, mesh=mesh, in_specs=in_specs, out_specs=out_specs, check_vma=False
    )
```

time: 448 us -> 79 us (0.18)
  the two profiles are of different devices: /device:TPU:48 before, /device:TPU:1 now
where the time goes in v2:
time: 79 us; the launch traced here: 78.7 us
  blocking collectives  54 us (68%)
  starting transfers between devices  15.3 us (19%)
  Pallas kernels  9.21 us (12%)
    all_gather x1, blocking collectives, per_device(): w_z = lax.all_gather(w_own, 'idx', axis=0, axis_index_groups=Z_GROUPS)  29.9 us
    all_to_all x1, blocking collectives, per_device(): lax.all_to_all(partial.reshape(-1, RP, NP), ('idx', 'rep'), split_axis=0,...  24.1 us
    all_to_all x1, starting transfers between devices, per_device(): lax.all_to_all(w_parts, 'rep', split_axis=0, concat_axis=0, tiled=True)  10.2 us
    pallas_call x1, Pallas kernels, per_device(): call(t_kernel, (XS * YS * CS, RP, 16 * KP), BF16, 4 * 10 ** 9, 4 * 10 **...  5.73 us
    all_to_all x1, starting transfers between devices, per_device(): lax.all_to_all(t_parts, ('idx', 'rep'), split_axis=0, concat_axis=0, axis...  5.12 us
    pallas_call x1, Pallas kernels, per_device(): call(w_kernel, (8, KP, NP), BF16, 10 ** 6, 2 * 10 ** 5, room=58, in_specs...  1.86 us
  transfers between devices with their start and end apart: 2, of which 0 were waited for; matrix products, arithmetic and copies ran while one was open for 0% of the time, Pallas kernels for 7%

profile of v2, /device:TPU:1, one launch (start us, length us, event | category | flops | bytes accessed | tf_op | source)
XLA Modules:
  0.0 78.7 jit_solution(12808578925722678202)
XLA Ops:
  0.0 1.9 %shard_map.91 = bf16[8,64,128]{2,1,0:T(8,128)(2,1)} custom-call(s32[512]{0:T(512)} %c_hbm.1, s32[4]{0:T(128)} %b_hbm.3, s32[1,100]{1,0:T(1,128)} %bitcast.8, bf16[400,100]{1,0:T(8,128)(2,1)} %bitcast.12), custom_call_target="tpu_custom_call" | custom-call | flops 1000000 | bytes 200000 | tf_op jit(solution)/shard_map/pallas_call | solution.py:202
  1.9 10.2 %all-to-all-start.1 = ((bf16[8,64,128]{2,1,0:T(8,128)(2,1)}), bf16[8,64,128]{2,1,0:T(8,128)(2,1)S(1)}, u32[]{:S(2)}, u32[]{:S(2)}) async-start(bf16[8,64,128]{2,1,0:T(8,128)(2,1)} %shard_map.91), calls=%async_computation.1 | async-start | bytes 262144 | tf_op jit(solution)/shard_map/all_to_all | solution.py:212
  12.0 5.7 %shard_map.92 = bf16[32,32,1024]{2,1,0:T(8,128)(2,1)} custom-call(s32[128]{0:T(128)} %a_hbm.3, s32[1,512]{1,0:T(1,128)} %bitcast.13, s32[1,100]{1,0:T(1,128)} %bitcast.9, bf16[25,51200]{1,0:T(8,128)(2,1)} %t_hbm.1), custom_call_target="tpu_custom_call" | custom-call | flops 4000000000 | bytes 4000000 | tf_op jit(solution)/shard_map/pallas_call | solution.py:214
  17.8 0.0 copy-start
  17.8 0.0 copy-start.1
  17.8 0.0 copy-start.2
  17.8 0.0 copy-start.3
  17.8 0.0 copy-start.4
  17.8 0.0 copy-start.5
  17.8 0.0 all-to-all-done.1
  17.8 5.1 %all-to-all-start = ((bf16[32,32,1024]{2,1,0:T(8,128)(2,1)}), bf16[32,32,1024]{2,1,0:T(8,128)(2,1)S(1)}, u32[]{:S(2)}, u32[]{:S(2)}) async-start(bf16[32,32,1024]{2,1,0:T(8,128)(2,1)} %shard_map.92), calls=%async_computation | async-start | bytes 4194304 | tf_op jit(solution)/shard_map/all_to_all | solution.py:231
  23.0 29.9 %all-gather.w_ref = bf16[1024,128]{1,0:T(8,128)(2,1)S(1)} all-gather(bf16[64,128]{1,0:T(8,128)(2,1)S(1)} %reduce_sum.9), channel_id=2, replica_groups={{0,8,16,24,32,40,48,56,64,72,80,88,96,104,112,120},{128,136,144,152,160..., dimensions={0}, use_global_device_ids=true | all-gather | bytes 278528 | tf_op jit(solution)/shard_map/all_gather | solution.py:236
  52.9 0.0 all-to-all-done
  52.9 0.0 copy-done
  52.9 0.0 copy-done.1
  52.9 0.0 copy-done.2
  52.9 0.0 copy-done.3
  52.9 0.0 copy-done.4
  52.9 0.0 copy-done.5
  52.9 0.9 %shard_map.93 = (f32[1024,128]{1,0:T(8,128)S(1)}, f32[25,400]{1,0:T(8,128)S(1)}, f32[25,400]{1,0:T(8,128)S(1)}) custom-call(bf16[1024,1024]{1,0:T(8,128)(2,1)S(1)} %bitcast.6, bf16[1024,128]{1,0:T(8,128)(2,1)S(1)} %all-gather.w_ref, s32[128]{0:T(128)S(1)} %copy-done.2, s32[4]{0:T(128)S(1)} %copy-done.1, f32[128]{0:T(128)S(1)} %copy-done.3, f32[4]{0:T(128)S(1)} %copy-done.4, ...), custom_call_target="tpu_custom_call" | custom-call | flops 268435456 | bytes 3000000 | tf_op jit(solution)/shard_map/pallas_call | solution.py:237
  53.9 24.1 %all_to_all.15.part_ref = f32[32,32,128]{2,1,0:T(8,128)S(1)} all-to-all(f32[32,32,128]{2,1,0:T(8,128)S(1)} %bitcast.7), channel_id=1, replica_groups={{0,1,2,3,4,5,6,7,128,129,130,131,132,133,134,135,256,257,258,259,260,26..., dimensions={0} | all-to-all | bytes 1048576 | tf_op jit(solution)/shard_map/all_to_all | solution.py:246
  78.0 0.7 shard_map.94
  (1 shorter events, 0.0 us)
Async XLA Ops:
  1.9 16.0 %all-to-all-start.1 = ((bf16[8,64,128]{2,1,0:T(8,128)(2,1)}), bf16[8,64,128]{2,1,0:T(8,128)(2,1)S(1)}, u32[]{:S(2)}, u32[]{:S(2)}) async-start(bf16[8,64,128]{2,1,0:T(8,128)(2,1)} %shard_map.91), calls=%async_computation.1 | async-start | bytes 262144 | tf_op jit(solution)/shard_map/all_to_all | solution.py:212
  17.8 35.1 %copy-start = (s32[100]{0:T(128)S(1)}, s32[100]{0:T(128)}, u32[]{:S(2)}) copy-start(s32[100]{0:T(128)} %param.14) | copy-start | bytes 1204
  17.8 35.1 %copy-start.1 = (s32[4]{0:T(128)S(1)}, s32[4]{0:T(128)}, u32[]{:S(2)}) copy-start(s32[4]{0:T(128)} %b_hbm.3) | copy-start | bytes 52
  17.8 35.1 %copy-start.2 = (s32[128]{0:T(128)S(1)}, s32[128]{0:T(128)}, u32[]{:S(2)}) copy-start(s32[128]{0:T(128)} %a_hbm.3) | copy-start | bytes 1540
  17.8 35.1 %copy-start.3 = (f32[128]{0:T(128)S(1)}, f32[128]{0:T(128)}, u32[]{:S(2)}) copy-start(f32[128]{0:T(128)} %ea_hbm.1) | copy-start | bytes 1540
  17.8 35.1 %copy-start.4 = (f32[4]{0:T(128)S(1)}, f32[4]{0:T(128)}, u32[]{:S(2)}) copy-start(f32[4]{0:T(128)} %eb_hbm.1) | copy-start | bytes 52
  17.8 35.1 %copy-start.5 = (f32[100]{0:T(128)S(1)}, f32[100]{0:T(128)}, u32[]{:S(2)}) copy-start(f32[100]{0:T(128)} %param.17) | copy-start | bytes 1204
  17.8 35.0 %all-to-all-start = ((bf16[32,32,1024]{2,1,0:T(8,128)(2,1)}), bf16[32,32,1024]{2,1,0:T(8,128)(2,1)S(1)}, u32[]{:S(2)}, u32[]{:S(2)}) async-start(bf16[32,32,1024]{2,1,0:T(8,128)(2,1)} %shard_map.92), calls=%async_computation | async-start | bytes 4194304 | tf_op jit(solution)/shard_map/all_to_all | solution.py:231

commit v3 on v2

--- a/solution.py
+++ b/solution.py
@@ -8,21 +8,28 @@
 O = 100
 G = 8
 COLS = 400
-KP = 64
 NP = 128
+KP = 128
 RP = 32
 ROWS = 25
 GROUP = G * O
 CHUNK = 4 * GROUP
 CHUNKS = 16
-STEP = 4
+PER_X = 4
 WINDOW = 896
 F32, BF16, I32 = jnp.float32, jnp.bfloat16, jnp.int32
 HBM = pl.BlockSpec(memory_space=pltpu.HBM)
 ZS, XS, YS, CS = 16, 4, 4, 2
 Z_GROUPS = [[x * ZS + z for z in range(ZS)] for x in range(XS)]
-PLANES = [
-    [(x * ZS + z) * YS * CS + p for x in range(XS) for p in range(YS * CS)] for z in range(ZS)
+CORE_PLANES = [
+    [(x * ZS + z) * YS * CS + y * CS + c for x in range(XS) for y in range(YS)]
+    for z in range(ZS)
+    for c in range(CS)
+]
+Z_CORE_GROUPS = [
+    [(x * ZS + z) * YS * CS + y * CS + c for z in range(ZS) for c in range(CS)]
+    for x in range(XS)
+    for y in range(YS)
 ]
 
 
@@ -66,30 +73,28 @@
         copy.wait()
 
 
-def w_kernel(c_hbm, b_hbm, occ_hbm, w_hbm, out_ref, c_irrep, b_irrep, occ, w_ref, flat, sems):
+def w_kernel(c_hbm, b_hbm, occ_hbm, w_hbm, out_ref, c_irrep, b_irrep, occ, w_ref, sems):
     fetch((c_hbm, b_hbm, occ_hbm, w_hbm), (c_irrep, b_irrep, occ, w_ref), sems)
-    occ_f = occ[...].astype(F32)
     s = iota((COLS, 1), 0)
     slab = jnp.full((COLS, 1), b_irrep[0], I32)
     for b in range(1, COLS // O):
         slab = jnp.where(s >= b * O, b_irrep[b], slab)
     hit = iota((COLS, O), 1) == mod_o(s)
-    col = slab ^ jnp.sum(jnp.where(hit, occ_f, 0.0), axis=1, keepdims=True).astype(I32)
+    col = slab ^ jnp.sum(jnp.where(hit, occ[...].astype(F32), 0.0), axis=1, keepdims=True).astype(I32)
     row = c_irrep[place()] ^ occ[...]
-    flat[...] = jnp.zeros_like(flat)
-    flat[:COLS, :O] = jnp.where(row == col, w_ref[...].astype(F32), 0.0)
-    for n in range(4):
-        part = flat[NP * n : NP * n + NP, :].T.astype(BF16)
-        for half in range(2):
-            out_ref[4 * half + n] = part[KP * half : KP * half + KP]
+    out_ref[...] = jnp.zeros_like(out_ref)
+    out_ref[:COLS, :O] = jnp.where(row == col, w_ref[...].astype(F32), 0.0).astype(BF16)
 
 
 def t_kernel(
-    a_hbm, c_hbm, occ_hbm, t_hbm, out_ref, a_irrep, c_lanes, occ, t_ref, want, have, pick, kept, sems, t_sems
+    a_hbm, c_hbm, occ_hbm, t_hbm, out_hbm, a_irrep, c_lanes, occ, t_ref, want, have, pick, kept, packed, sems, t_sems, o_sems
 ):
     def block(q):
         lanes = pl.ds(CHUNK * q, CHUNK)
         return pltpu.make_async_copy(t_hbm.at[:, lanes], t_ref.at[:, lanes], t_sems.at[q])
+
+    def send(x, y):
+        return pltpu.make_async_copy(packed.at[x], out_hbm.at[YS * x + y], o_sems.at[YS * x + y])
 
     small = [
         pltpu.make_async_copy(s, t, sems.at[i])
@@ -102,7 +107,7 @@
     for j in range(4):
         at = iota((WINDOW, 1), 0) - 32 * j
         k = jnp.where((at >= 0) & (at < GROUP), mod_o(jnp.maximum(at, 0)), -1)
-        pick[j] = jnp.where(k == iota((WINDOW, 128), 1), 1.0, 0.0).astype(BF16)
+        pick[j] = jnp.where(k == iota((WINDOW, KP), 1), 1.0, 0.0).astype(BF16)
     fold = jnp.where(iota((512, 128), 0) % 32 == iota((512, 128), 1), 1.0, 0.0).astype(BF16)
     lane = iota((128, CHUNK), 1)
     first = O * iota((128, 1), 0)
@@ -119,29 +124,23 @@
     mine = jnp.where(iota(shape, 1) // 32 == iota(shape, 0), c_lanes[...].astype(F32), 0.0)
     rows = jnp.dot(mine.astype(BF16), fold, preferred_element_type=F32).astype(BF16)
     have[...] = jnp.dot(rows, spread, preferred_element_type=F32)
-    for q in range(CHUNKS):
-        block(q).wait()
-        mask = want[:ROWS, :] == have[q : q + 1, :].astype(BF16)
-        got = t_ref[:, CHUNK * q : CHUNK * (q + 1)]
-        kept[RP * q : RP * q + ROWS, :] = jnp.where(mask, got, jnp.zeros((), BF16))
-    low = iota((CHUNKS * RP, 128), 1) < KP
-    for pair in range(2):
-        even, odd = (
-            jnp.dot(kept[:, 768 * j : 768 * j + WINDOW], pick[j], preferred_element_type=F32)
-            for j in (2 * pair, 2 * pair + 1)
-        )
-        halves = (
-            jnp.where(low, even, pltpu.roll(odd, KP, 1)),
-            jnp.where(low, pltpu.roll(even, KP, 1), odd),
-        )
-        for half in range(2):
-            packed = halves[half].astype(BF16)
-            for q in range(CHUNKS):
-                x, h = divmod(q, CHUNKS // XS)
-                lanes = slice(256 * h + 128 * pair, 256 * h + 128 * pair + 128)
-                part = packed[RP * q : RP * q + RP]
-                for n in range(4):
-                    out_ref[YS * CS * x + 4 * half + n, :, lanes] = part
+    for x in range(XS):
+        part = slice(RP * PER_X * x, RP * PER_X * (x + 1))
+        for q in range(PER_X * x, PER_X * (x + 1)):
+            block(q).wait()
+            mask = want[:ROWS, :] == have[q : q + 1, :].astype(BF16)
+            got = t_ref[:, CHUNK * q : CHUNK * (q + 1)]
+            kept[RP * q : RP * q + ROWS, :] = jnp.where(mask, got, jnp.zeros((), BF16))
+        for j in range(4):
+            full = jnp.dot(kept[part, 768 * j : 768 * j + WINDOW], pick[j], preferred_element_type=F32)
+            for h in range(PER_X):
+                lanes = slice(KP * (4 * h + j), KP * (4 * h + j + 1))
+                packed[x, :, lanes] = full[RP * h : RP * (h + 1)].astype(BF16)
+        for y in range(YS):
+            send(x, y).start()
+    for x in range(XS):
+        for y in range(YS):
+            send(x, y).wait()
 
 
 def mm_kernel(
@@ -156,7 +155,10 @@
     ]
     for copy in copies:
         copy.start()
-    out_ref[...] = jnp.dot(t_ref[...], w_ref[...], preferred_element_type=F32)
+    w_t = jnp.concatenate([w_ref[z] for z in range(ZS)], axis=1)
+    out_ref[...] = lax.dot_general(
+        t_ref[...], w_t, (((1,), (1,)), ((), ())), preferred_element_type=F32
+    )
     for copy in copies:
         copy.wait()
     here = place()
@@ -172,11 +174,9 @@
 def end_kernel(energy_ref, same_ref, part_ref, out_ref):
     for n in range(4):
         lo, hi = NP * n, min(NP * n + NP, COLS)
-        total = None
-        for x in range(XS):
-            for half in range(2):
-                part = part_ref[YS * CS * x + 4 * half + n, :ROWS, : hi - lo]
-                total = part if total is None else total + part
+        total = part_ref[n, :ROWS, : hi - lo]
+        for x in range(1, XS):
+            total = total + part_ref[YS * x + n, :ROWS, : hi - lo]
         total = jnp.where(same_ref[:, lo:hi] > 0.5, total, 0.0)
         out_ref[:, lo:hi] = total / energy_ref[:, lo:hi]
 
@@ -200,21 +200,19 @@
     whole = pl.BlockSpec(memory_space=pltpu.VMEM)
     occ, eo = occ_irrep.reshape(1, O), eps_occ.reshape(1, O)
     w_parts = call(
-        w_kernel, (8, KP, NP), BF16, 10**6, 2 * 10**5, room=58,
+        w_kernel, (4 * NP, KP), BF16, 10**6, 2 * 10**5, room=58,
         in_specs=[HBM] * 4,
         out_specs=whole,
-        scratch_shapes=[
-            smem((512,), I32), smem((4,), I32), vmem((1, O), I32), vmem((COLS, O), BF16),
-            vmem((4 * NP, 2 * KP), F32), dma((4,)),
-        ],
+        scratch_shapes=[smem((512,), I32), smem((4,), I32), vmem((1, O), I32), vmem((COLS, O), BF16), dma((4,))],
     )(c_irrep, b_irrep, occ, w_cycle.T)
     occ_late, w_parts = lax.optimization_barrier((occ, w_parts))
+    w_parts = w_parts.reshape(8, NP // 2, KP)
     w_got = lax.all_to_all(w_parts, "rep", split_axis=0, concat_axis=0, tiled=True)
     w_own = jnp.sum(w_got, axis=0, dtype=BF16)
     t_parts = call(
-        t_kernel, (XS * YS * CS, RP, 16 * KP), BF16, 4 * 10**9, 4 * 10**6, room=58,
+        t_kernel, (XS * YS, RP, ZS * KP), BF16, 4 * 10**9, 4 * 10**6, room=58,
         in_specs=[HBM] * 4,
-        out_specs=whole,
+        out_specs=HBM,
         scratch_shapes=[
             smem((128,), I32),
             vmem((1, 512), I32),
@@ -222,30 +220,32 @@
             vmem((ROWS, CHUNKS * CHUNK), BF16),
             vmem((RP, CHUNK), BF16),
             vmem((CHUNKS, CHUNK), F32),
-            vmem((4, WINDOW, 128), BF16),
+            vmem((4, WINDOW, KP), BF16),
             vmem((CHUNKS * RP, CHUNK), BF16),
+            vmem((XS, RP, ZS * KP), BF16),
             dma((3,)),
             dma((CHUNKS,)),
+            dma((XS * YS,)),
         ],
     )(a_irrep, c_irrep.reshape(1, 512), occ_late, t_slab)
     t_got = lax.all_to_all(
-        t_parts, ("idx", "rep"), split_axis=0, concat_axis=0, axis_index_groups=PLANES, tiled=True
+        t_parts, ("idx", "rep"), split_axis=0, concat_axis=0, axis_index_groups=CORE_PLANES, tiled=True
     )
 
     w_own, t_parts = lax.optimization_barrier((w_own, t_parts))
-    w_z = lax.all_gather(w_own, "idx", axis=0, axis_index_groups=Z_GROUPS)
+    w_z = lax.all_gather(w_own, ("idx", "rep"), axis=0, axis_index_groups=Z_CORE_GROUPS)
     partial, energy, same = call(
-        mm_kernel, [(XS * YS * CS * RP, NP), (ROWS, COLS), (ROWS, COLS)], F32, 2 * 1024 * 1024 * 128, 3 * 10**6, room=24,
+        mm_kernel, [(XS * YS * RP, NP), (ROWS, COLS), (ROWS, COLS)], F32, 2 * 512 * 2048 * 128, 3 * 10**6, room=24,
         in_specs=[whole] * 2 + [HBM] * 6,
         out_specs=[whole] * 3,
         scratch_shapes=[
             smem((128,), I32), smem((4,), I32), smem((128,), F32), smem((4,), F32),
             vmem((1, O), I32), vmem((1, O), F32), dma((6,)),
         ],
-    )(t_got.reshape(-1, 16 * KP), w_z.reshape(ZS * KP, NP), a_irrep, b_irrep, eps_a, eps_b, occ, eo)
+    )(t_got.reshape(-1, ZS * KP), w_z.reshape(ZS, NP, KP), a_irrep, b_irrep, eps_a, eps_b, occ, eo)
     ends = lax.all_to_all(
         partial.reshape(-1, RP, NP), ("idx", "rep"), split_axis=0, concat_axis=0,
-        axis_index_groups=PLANES, tiled=True,
+        axis_index_groups=CORE_PLANES, tiled=True,
     )
     return call(
         end_kernel, (ROWS, COLS), F32, 10**6, 10**6, room=24, in_specs=[whole] * 3, out_specs=whole

time: 79 us -> 74.9 us (0.948)
  blocking collectives: 54 us -> 50.9 us
    all_to_all x1, blocking collectives: 24.1 us -> 14.5 us  [per_device(): lax.all_to_all(partial.reshape(-1, RP, NP), ('idx', 'rep'), split_axis=0,...]
    all_gather x1, blocking collectives: 29.9 us -> 36.4 us  [per_device(): lax.all_gather(w_own, ('idx', 'rep'), axis=0, axis_index_groups=Z_CORE_GR...]
where the time goes in v3:
time: 74.9 us; the launch traced here: 74.5 us
  blocking collectives  50.9 us (68%)
  starting transfers between devices  14.6 us (19%)
  Pallas kernels  8.83 us (12%)
    all_gather x1, blocking collectives, per_device(): lax.all_gather(w_own, ('idx', 'rep'), axis=0, axis_index_groups=Z_CORE_GR...  36.4 us
    all_to_all x1, blocking collectives, per_device(): lax.all_to_all(partial.reshape(-1, RP, NP), ('idx', 'rep'), split_axis=0,...  14.5 us
    all_to_all x1, starting transfers between devices, per_device(): lax.all_to_all(w_parts, 'rep', split_axis=0, concat_axis=0, tiled=True)  10.2 us
    pallas_call x1, Pallas kernels, per_device(): call(t_kernel, (XS * YS, RP, ZS * KP), BF16, 4 * 10 ** 9, 4 * 10 ** 6, ro...  5.46 us
    all_to_all x1, starting transfers between devices, per_device(): lax.all_to_all(t_parts, ('idx', 'rep'), split_axis=0, concat_axis=0, axis...  4.43 us
    pallas_call x1, Pallas kernels, per_device(): call(w_kernel, (4 * NP, KP), BF16, 10 ** 6, 2 * 10 ** 5, room=58, in_spec...  1.76 us
  transfers between devices with their start and end apart: 2, of which 0 were waited for; matrix products, arithmetic and copies ran while one was open for 0% of the time, Pallas kernels for 7%

profile of v3, /device:TPU:1, one launch (start us, length us, event | category | flops | bytes accessed | tf_op | source)
XLA Modules:
  0.0 74.5 jit_solution(14037299521036830781)
XLA Ops:
  0.0 1.8 %shard_map.91 = bf16[512,128]{1,0:T(8,128)(2,1)} custom-call(s32[512]{0:T(512)} %c_hbm.1, s32[4]{0:T(128)} %b_hbm.3, s32[1,100]{1,0:T(1,128)} %bitcast.11, bf16[400,100]{1,0:T(8,128)(2,1)} %bitcast.16), custom_call_target="tpu_custom_call" | custom-call | flops 1000000 | bytes 200000 | tf_op jit(solution)/shard_map/pallas_call | solution.py:202
  1.8 10.2 %all-to-all-start.1 = ((bf16[8,64,128]{2,1,0:T(8,128)(2,1)}), bf16[8,64,128]{2,1,0:T(8,128)(2,1)S(1)}, u32[]{:S(2)}, u32[]{:S(2)}) async-start(bf16[8,64,128]{2,1,0:T(8,128)(2,1)} %bitcast.15), calls=%async_computation.1 | async-start | bytes 262144 | tf_op jit(solution)/shard_map/all_to_all | solution.py:210
  11.9 5.5 %shard_map.92 = bf16[16,32,2048]{2,1,0:T(8,128)(2,1)} custom-call(s32[128]{0:T(128)} %a_hbm.3, s32[1,512]{1,0:T(1,128)} %bitcast.17, s32[1,100]{1,0:T(1,128)} %bitcast.12, bf16[25,51200]{1,0:T(8,128)(2,1)} %t_hbm.1), custom_call_target="tpu_custom_call" | custom-call | flops 4000000000 | bytes 4000000 | tf_op jit(solution)/shard_map/pallas_call | solution.py:212
  17.4 0.0 copy-start
  17.4 0.0 copy-start.1
  17.4 0.0 copy-start.2
  17.4 0.0 copy-start.3
  17.5 0.0 copy-start.4
  17.5 0.0 copy-start.5
  17.5 0.0 all-to-all-done.1
  17.5 4.4 %all-to-all-start = ((bf16[16,32,2048]{2,1,0:T(8,128)(2,1)}), bf16[16,32,2048]{2,1,0:T(8,128)(2,1)S(1)}, u32[]{:S(2)}, u32[]{:S(2)}) async-start(bf16[16,32,2048]{2,1,0:T(8,128)(2,1)} %shard_map.92), calls=%async_computation | async-start | bytes 4194304 | tf_op jit(solution)/shard_map/all_to_all | solution.py:231
  22.0 36.4 %all-gather = bf16[2048,128]{1,0:T(8,128)(2,1)S(1)} all-gather(bf16[64,128]{1,0:T(8,128)(2,1)S(1)} %reduce_sum.9), channel_id=2, replica_groups={{0,1,8,9,16,17,24,25,32,33,40,41,48,49,56,57,64,65,72,73,80,81,88,89,96..., dimensions={0}, use_global_device_ids=true | all-gather | bytes 540672 | tf_op jit(solution)/shard_map/all_gather | solution.py:236
  58.4 0.0 all-to-all-done
  58.4 0.0 copy-done
  58.4 0.0 copy-done.1
  58.4 0.0 copy-done.2
  58.4 0.0 copy-done.3
  58.4 0.0 copy-done.4
  58.4 0.0 copy-done.5
  58.4 0.9 %shard_map.93 = (f32[512,128]{1,0:T(8,128)S(1)}, f32[25,400]{1,0:T(8,128)S(1)}, f32[25,400]{1,0:T(8,128)S(1)}) custom-call(bf16[512,2048]{1,0:T(8,128)(2,1)S(1)} %bitcast.8, bf16[16,128,128]{2,1,0:T(8,128)(2,1)S(1)} %bitcast.9, s32[128]{0:T(128)S(1)} %copy-done.2, s32[4]{0:T(128)S(1)} %copy-done.1, f32[128]{0:T(128)S(1)} %copy-done.3, f32[4]{0:T(128)S(1)} %copy-done.4, ...), custom_call_target="tpu_custom_call" | custom-call | flops 268435456 | bytes 3000000 | tf_op jit(solution)/shard_map/pallas_call | solution.py:237
  59.4 14.5 %all_to_all.15.part_ref = f32[16,32,128]{2,1,0:T(8,128)S(1)} all-to-all(f32[16,32,128]{2,1,0:T(8,128)S(1)} %bitcast.10), channel_id=1, replica_groups={{0,2,4,6,128,130,132,134,256,258,260,262,384,386,388,390},{1,3,5,7,129,..., dimensions={0} | all-to-all | bytes 524288 | tf_op jit(solution)/shard_map/all_to_all | solution.py:246
  73.9 0.7 shard_map.94
  (1 shorter events, 0.0 us)
Async XLA Ops:
  1.8 15.7 %all-to-all-start.1 = ((bf16[8,64,128]{2,1,0:T(8,128)(2,1)}), bf16[8,64,128]{2,1,0:T(8,128)(2,1)S(1)}, u32[]{:S(2)}, u32[]{:S(2)}) async-start(bf16[8,64,128]{2,1,0:T(8,128)(2,1)} %bitcast.15), calls=%async_computation.1 | async-start | bytes 262144 | tf_op jit(solution)/shard_map/all_to_all | solution.py:210
  17.4 41.0 %copy-start = (s32[100]{0:T(128)S(1)}, s32[100]{0:T(128)}, u32[]{:S(2)}) copy-start(s32[100]{0:T(128)} %param.14) | copy-start | bytes 1204
  17.4 41.0 %copy-start.1 = (s32[4]{0:T(128)S(1)}, s32[4]{0:T(128)}, u32[]{:S(2)}) copy-start(s32[4]{0:T(128)} %b_hbm.3) | copy-start | bytes 52
  17.4 41.0 %copy-start.2 = (s32[128]{0:T(128)S(1)}, s32[128]{0:T(128)}, u32[]{:S(2)}) copy-start(s32[128]{0:T(128)} %a_hbm.3) | copy-start | bytes 1540
  17.4 41.0 %copy-start.3 = (f32[128]{0:T(128)S(1)}, f32[128]{0:T(128)}, u32[]{:S(2)}) copy-start(f32[128]{0:T(128)} %ea_hbm.1) | copy-start | bytes 1540
  17.5 41.0 %copy-start.4 = (f32[4]{0:T(128)S(1)}, f32[4]{0:T(128)}, u32[]{:S(2)}) copy-start(f32[4]{0:T(128)} %eb_hbm.1) | copy-start | bytes 52
  17.5 40.9 %copy-start.5 = (f32[100]{0:T(128)S(1)}, f32[100]{0:T(128)}, u32[]{:S(2)}) copy-start(f32[100]{0:T(128)} %param.17) | copy-start | bytes 1204
  17.5 40.9 %all-to-all-start = ((bf16[16,32,2048]{2,1,0:T(8,128)(2,1)}), bf16[16,32,2048]{2,1,0:T(8,128)(2,1)S(1)}, u32[]{:S(2)}, u32[]{:S(2)}) async-start(bf16[16,32,2048]{2,1,0:T(8,128)(2,1)} %shard_map.92), calls=%async_computation | async-start | bytes 4194304 | tf_op jit(solution)/shard_map/all_to_all | solution.py:231

commit v4 on v3

v4 whole, which is shorter than its diff:
```python
import jax
import jax.numpy as jnp
from jax import lax
from jax.experimental import pallas as pl
from jax.experimental.pallas import tpu as pltpu
from jax.sharding import PartitionSpec as P

O = 100
G = 8
COLS = 400
NP = 128
KP = 128
RP = 32
ROWS = 25
GROUP = G * O
CHUNK = 4 * GROUP
CHUNKS = 16
PER_X = 4
WINDOW = 896
F32, BF16, I32 = jnp.float32, jnp.bfloat16, jnp.int32
HBM = pl.BlockSpec(memory_space=pltpu.HBM)
ZS, XS, YS, CS = 16, 4, 4, 2
Z_GROUPS = [[x * ZS + z for z in range(ZS)] for x in range(XS)]
CORE_PLANES = [
    [(x * ZS + z) * YS * CS + y * CS + c for x in range(XS) for y in range(YS)]
    for z in range(ZS)
    for c in range(CS)
]
Z_CORE_GROUPS = [
    [(x * ZS + z) * YS * CS + y * CS + c for z in range(ZS) for c in range(CS)]
    for x in range(XS)
    for y in range(YS)
]


def iota(shape, dim):
    return lax.broadcasted_iota(I32, shape, dim)


def mod_o(n):
    return n - O * jnp.floor((n.astype(F32) + 0.5) * (1.0 / O)).astype(I32)


def to_rows(lanes, count, first):
    shape = (count, lanes.shape[1])
    hit = iota(shape, 1) == iota(shape, 0) + first
    return jnp.sum(jnp.where(hit, lanes, 0.0), axis=1, keepdims=True)


def lookup(lanes, index):
    parts = [
        jnp.take_along_axis(lanes, index[:, at : at + 128], axis=1) for at in range(0, index.shape[1], 128)
    ]
    return jnp.concatenate(parts, axis=1)


def by_slab(ref, dtype):
    s = iota((8, 4 * NP), 1)
    out = jnp.full((8, 4 * NP), ref[0, 0], dtype)
    for b in range(1, COLS // O):
        out = jnp.where(s >= b * O, ref[0, b], out)
    return out


def fetch(sources, targets, sems):
    copies = [pltpu.make_async_copy(s, t, sems.at[i]) for i, (s, t) in enumerate(zip(sources, targets))]
    for copy in copies:
        copy.start()
    return copies


def place():
    return lax.axis_index("idx") * (YS * CS) + lax.axis_index("rep")


def padded(lanes):
    wide = jnp.concatenate([lanes, jnp.zeros((1, 128 - O), lanes.dtype)], axis=1)
    return jnp.broadcast_to(wide, (8, 128))


def head_kernel(b_hbm, c_hbm, occ_hbm, w_hbm, t_hbm, out_hbm, t_ref, b_irrep, c_irrep, occ, w_ref, out_ref, sems, t_sem, out_sem):
    copies = fetch((b_hbm, c_hbm, occ_hbm, w_hbm), (b_irrep, c_irrep, occ, w_ref), sems)
    whole_t = pltpu.make_async_copy(t_hbm, t_ref, t_sem)
    whole_t.start()
    out_ref[...] = jnp.zeros_like(out_ref)
    s = iota((COLS, 1), 0)
    hit = iota((COLS, O), 1) == mod_o(s)
    for copy in copies:
        copy.wait()
    slab = jnp.full((COLS, 1), b_irrep[0, 0], I32)
    for b in range(1, COLS // O):
        slab = jnp.where(s >= b * O, b_irrep[0, b], slab)
    col = slab ^ jnp.sum(jnp.where(hit, occ[...].astype(F32), 0.0), axis=1, keepdims=True).astype(I32)
    row = c_irrep[0, place()] ^ occ[...]
    out_ref[:COLS, :O] = jnp.where(row == col, w_ref[...].astype(F32), 0.0).astype(BF16)
    send = pltpu.make_async_copy(out_ref, out_hbm, out_sem)
    send.start()
    send.wait()
    whole_t.wait()


def t_kernel(
    a_hbm, c_hbm, occ_hbm, b_hbm, ea_hbm, eb_hbm, eo_hbm, t_ref, out_hbm, energy, same,
    a_irrep, c_lanes, occ, b_irrep, eps_a, eps_b, eps_occ, want, have, pick, kept, packed, sems, o_sems,
):
    def send(x, y):
        return pltpu.make_async_copy(packed.at[x], out_hbm.at[YS * x + y], o_sems.at[YS * x + y])

    copies = fetch(
        (a_hbm, c_hbm, occ_hbm, b_hbm, ea_hbm, eb_hbm, eo_hbm),
        (a_irrep, c_lanes, occ, b_irrep, eps_a, eps_b, eps_occ),
        sems,
    )
    at = iota((WINDOW + 96, 1), 0) - 96
    k = jnp.where((at >= 0) & (at < GROUP), mod_o(jnp.maximum(at, 0)), -1)
    pick[...] = jnp.where(k == iota((WINDOW + 96, KP), 1), 1.0, 0.0).astype(BF16)
    for q in range(CHUNKS):
        kept[RP * q + 16 : RP * q + RP, :] = jnp.zeros((16, CHUNK), BF16)
    lane = iota((8, CHUNK), 1)
    mod = mod_o(lane)
    over = (lane - mod) // O
    group = iota((8, 128), 0) // 4
    for copy in copies:
        copy.wait()
    here = place()
    a, first = here // 4, ROWS * (here % 4)
    row = a_irrep[0, a] ^ to_rows(occ[...].astype(F32), RP, first).astype(I32)
    occ_t = lookup(padded(occ[...]), mod)
    want[...] = (row ^ occ_t[:1]).astype(BF16)
    for half in range(2):
        lanes = [jnp.broadcast_to(c_lanes[:, 128 * v : 128 * v + 128], (8, 128)) for v in (2 * half, 2 * half + 1)]
        source = jnp.where(group == 0, lanes[0], lanes[1])
        have[8 * half : 8 * half + 8, :] = lookup(source, 32 * (iota((8, CHUNK), 0) % 4) + over).astype(F32)
    for x in range(XS):
        part = slice(RP * PER_X * x, RP * PER_X * (x + 1))
        for q in range(PER_X * x, PER_X * (x + 1)):
            mask = want[:ROWS, :] == have[q : q + 1, :].astype(BF16)
            got = t_ref[:, CHUNK * q : CHUNK * (q + 1)]
            kept[RP * q : RP * q + ROWS, :] = jnp.where(mask, got, jnp.zeros((), BF16))
        for j in range(4):
            full = jnp.dot(
                kept[part, 768 * j : 768 * j + WINDOW],
                pick[96 - 32 * j : 96 - 32 * j + WINDOW, :],
                preferred_element_type=F32,
            )
            for h in range(PER_X):
                lanes = slice(KP * (4 * h + j), KP * (4 * h + j + 1))
                packed[x, :, lanes] = full[RP * h : RP * (h + 1)].astype(BF16)
        for y in range(YS):
            send(x, y).start()
    wide = 4 * NP
    col = (by_slab(b_irrep, I32) ^ occ_t[:, :wide])[:1, :COLS]
    column_energy = (by_slab(eps_b, F32) - lookup(padded(eps_occ[...]), mod[:, :wide]))[:1, :COLS]
    energy[...] = (eps_a[0, a] - to_rows(eps_occ[...], ROWS, first)) + column_energy
    same[...] = jnp.where(row[:ROWS] == col, 1.0, 0.0)
    for x in range(XS):
        for y in range(YS):
            send(x, y).wait()


def mm_kernel(t_ref, w_ref, out_ref):
    w_t = jnp.concatenate([w_ref[z] for z in range(ZS)], axis=1)
    out_ref[...] = lax.dot_general(
        t_ref[...], w_t, (((1,), (1,)), ((), ())), preferred_element_type=F32
    )


def end_kernel(energy_ref, same_ref, part_ref, out_ref):
    for n in range(4):
        lo, hi = NP * n, min(NP * n + NP, COLS)
        total = part_ref[n, :ROWS, : hi - lo]
        for x in range(1, XS):
            total = total + part_ref[YS * x + n, :ROWS, : hi - lo]
        total = jnp.where(same_ref[:, lo:hi] > 0.5, total, 0.0)
        out_ref[:, lo:hi] = total / energy_ref[:, lo:hi]


def call(kernel, out, flops, moved, room, **rest):
    return pl.pallas_call(
        kernel,
        out_shape=out,
        cost_estimate=pl.CostEstimate(flops=flops, bytes_accessed=moved, transcendentals=0),
        compiler_params=pltpu.CompilerParams(vmem_limit_bytes=room * 2**20),
        **rest,
    )


def per_device(t_slab, w_cycle, a_irrep, b_irrep, c_irrep, occ_irrep, eps_a, eps_b, eps_occ):
    vmem, smem, dma = pltpu.VMEM, pltpu.SMEM, pltpu.SemaphoreType.DMA
    struct = jax.ShapeDtypeStruct
    whole = pl.BlockSpec(memory_space=pltpu.VMEM)
    lanes = lambda vector: vector.reshape(1, -1)
    a_row, b_row, c_row, occ, eo = (lanes(v) for v in (a_irrep, b_irrep, c_irrep, occ_irrep, eps_occ))
    w_parts, t_near = call(
        head_kernel,
        [pltpu.HBM((4 * NP, KP), BF16), vmem((ROWS, CHUNKS * CHUNK), BF16)],
        10**7, 10**6, 56,
        in_specs=[HBM] * 5,
        out_specs=[HBM, whole],
        scratch_shapes=[
            smem((1, 4), I32), smem((1, 512), I32), vmem((1, O), I32), vmem((COLS, O), BF16),
            vmem((4 * NP, KP), BF16), dma((4,)), dma, dma,
        ],
    )(b_row, c_row, occ, w_cycle.T, t_slab)
    w_got = lax.all_to_all(w_parts.reshape(8, NP // 2, KP), "rep", split_axis=0, concat_axis=0, tiled=True)
    w_own = jnp.sum(w_got, axis=0, dtype=BF16)
    t_parts, energy, same = call(
        t_kernel,
        [pltpu.HBM((XS * YS, RP, ZS * KP), BF16), struct((ROWS, COLS), F32), struct((ROWS, COLS), F32)],
        4 * 10**9, 4 * 10**6, 55,
        in_specs=[HBM] * 7 + [whole],
        out_specs=[HBM, whole, whole],
        scratch_shapes=[
            smem((1, 128), I32), vmem((1, 512), I32), vmem((1, O), I32), smem((1, 4), I32), smem((1, 128), F32),
            smem((1, 4), F32), vmem((1, O), F32), vmem((RP, CHUNK), BF16), vmem((CHUNKS, CHUNK), F32),
            vmem((WINDOW + 96, KP), BF16), vmem((CHUNKS * RP, CHUNK), BF16), vmem((XS, RP, ZS * KP), BF16),
            dma((7,)), dma((XS * YS,)),
        ],
    )(
        a_row, c_row, occ, b_row, lanes(eps_a), lanes(eps_b), eo,
        pltpu.with_memory_space_constraint(t_near, pltpu.VMEM),
    )
    t_got = lax.all_to_all(
        t_parts, ("idx", "rep"), split_axis=0, concat_axis=0, axis_index_groups=CORE_PLANES, tiled=True
    )
    w_own, t_parts = lax.optimization_barrier((w_own, t_parts))
    w_z = lax.all_gather(w_own, ("idx", "rep"), axis=0, axis_index_groups=Z_CORE_GROUPS)
    partial = call(
        mm_kernel, struct((XS * YS * RP, NP), F32), 2 * 512 * 2048 * 128, 3 * 10**6, 24,
        in_specs=[whole] * 2, out_specs=whole,
    )(t_got.reshape(-1, ZS * KP), w_z.reshape(ZS, NP, KP))
    ends = lax.all_to_all(
        partial.reshape(-1, RP, NP), ("idx", "rep"), split_axis=0, concat_axis=0,
        axis_index_groups=CORE_PLANES, tiled=True,
    )
    return call(
        end_kernel, struct((ROWS, COLS), F32), 10**6, 10**6, 24, in_specs=[whole] * 3, out_specs=whole
    )(energy, same, ends)


def solution(mesh):
    in_specs = (P(("idx", "rep"), None), P(("idx", "rep"), None), P(), P(), P(), P(), P(), P(), P())
    out_specs = P(("idx", "rep"), None)
    return jax.shard_map(
        per_device, mesh=mesh, in_specs=in_specs, out_specs=out_specs, check_vma=False
    )
```

time: 74.9 us -> 73.2 us (0.977)
  Pallas kernels: 8.83 us -> 7.22 us
  waiting for transfers between devices: 0.01 us -> 1.49 us
  blocking collectives: 50.9 us -> 50 us
    pallas_call x4, Pallas kernels: 8.83 us -> 7.22 us  [the longest x1 3.8 us: per_device(): call(t_kernel, [pltpu.HBM((XS * YS, RP, ZS * KP), BF16), struct((ROWS, CO...]
    all_to_all x1, waiting for transfers between devices: 0.01 us -> 1.49 us  [per_device(): lax.all_to_all(w_parts.reshape(8, NP // 2, KP), 'rep', split_axis=0, conc...]
    all_gather x1, blocking collectives: 36.4 us -> 35.5 us  [per_device(): lax.all_gather(w_own, ('idx', 'rep'), axis=0, axis_index_groups=Z_CORE_GR...]
  transfers between devices with their start and end apart: 2 -> 2, of which waited for: 0 -> 1; matrix products, arithmetic and copies ran while one was open for 0% -> 0% of each run, Pallas kernels for 7% -> 5%
where the time goes in v4:
time: 73.2 us; the launch traced here: 72.8 us
  blocking collectives  50 us (68%)
  starting transfers between devices  14 us (19%)
  Pallas kernels  7.22 us (10%)
  waiting for transfers between devices  1.49 us (2%)
    all_gather x1, blocking collectives, per_device(): lax.all_gather(w_own, ('idx', 'rep'), axis=0, axis_index_groups=Z_CORE_GR...  35.5 us
    all_to_all x1, blocking collectives, per_device(): lax.all_to_all(partial.reshape(-1, RP, NP), ('idx', 'rep'), split_axis=0,...  14.5 us
    all_to_all x1, starting transfers between devices, per_device(): lax.all_to_all(w_parts.reshape(8, NP // 2, KP), 'rep', split_axis=0, conc...  10.2 us
    all_to_all x1, starting transfers between devices, per_device(): lax.all_to_all(t_parts, ('idx', 'rep'), split_axis=0, concat_axis=0, axis...  3.85 us
    pallas_call x1, Pallas kernels, per_device(): call(t_kernel, [pltpu.HBM((XS * YS, RP, ZS * KP), BF16), struct((ROWS, CO...  3.8 us
    pallas_call x1, Pallas kernels, per_device(): call(head_kernel, [pltpu.HBM((4 * NP, KP), BF16), vmem((ROWS, CHUNKS * CH...  2.06 us
    all_to_all x1, waiting for transfers between devices, per_device(): lax.all_to_all(w_parts.reshape(8, NP // 2, KP), 'rep', split_axis=0, conc...  1.49 us
  transfers between devices with their start and end apart: 2, of which 1 were waited for; matrix products, arithmetic and copies ran while one was open for 0% of the time, Pallas kernels for 5%

profile of v4, /device:TPU:1, one launch (start us, length us, event | category | flops | bytes accessed | tf_op | source)
XLA Modules:
  0.0 72.8 jit_solution(4709753186341850289)
XLA Ops:
  0.0 2.1 %shard_map.91 = (bf16[512,128]{1,0:T(8,128)(2,1)}, bf16[25,51200]{1,0:T(8,128)(2,1)S(1)}) custom-call(s32[1,4]{1,0:T(1,128)} %bitcast.21, s32[1,512]{1,0:T(1,128)} %bitcast.17, s32[1,100]{1,0:T(1,128)} %bitcast.19, bf16[400,100]{1,0:T(8,128)(2,1)} %bitcast.16, bf16[25,51200]{1,0:T(8,128)(2,1)} %t_hbm.1), custom_call_target="tpu_custom_call" | custom-call | flops 10000000 | bytes 1000000 | tf_op jit(solution)/shard_map/pallas_call | solution.py:194
  2.1 10.2 %all-to-all-start.1 = ((bf16[8,64,128]{2,1,0:T(8,128)(2,1)}), bf16[8,64,128]{2,1,0:T(8,128)(2,1)S(1)}, u32[]{:S(2)}, u32[]{:S(2)}) async-start(bf16[8,64,128]{2,1,0:T(8,128)(2,1)} %bitcast.15), calls=%async_computation.1 | async-start | bytes 262144 | tf_op jit(solution)/shard_map/all_to_all | solution.py:205
  12.2 3.8 %shard_map.92 = (bf16[16,32,2048]{2,1,0:T(8,128)(2,1)}, f32[25,400]{1,0:T(8,128)}, f32[25,400]{1,0:T(8,128)}) custom-call(s32[1,128]{1,0:T(1,128)} %bitcast.23, s32[1,512]{1,0:T(1,128)} %bitcast.18, s32[1,100]{1,0:T(1,128)} %bitcast.20, s32[1,4]{1,0:T(1,128)} %bitcast.22, f32[1,128]{1,0:T(1,128)} %bitcast.24, f32[1,4]{1,0:T(1,128)} %bitcast.25, ...), custom_call_target="tpu_custom_call" | custom-call | flops 4000000000 | bytes 4000000 | tf_op jit(solution)/shard_map/pallas_call | solution.py:207
  16.0 1.5 %all-to-all-done.1 = bf16[8,64,128]{2,1,0:T(8,128)(2,1)S(1)} async-done(((bf16[8,64,128]{2,1,0:T(8,128)(2,1)}), bf16[8,64,128]{2,1,0:T(8,128)(2,1)S(1)}, u32[]{:S(2)}, u32[]{:S(2)}) %all-to-all-start.1) | async-done | bytes 131104 | tf_op jit(solution)/shard_map/all_to_all | solution.py:205
  17.5 0.0 copy-start
  17.5 0.0 copy-start.1
  17.5 3.8 %all-to-all-start = ((bf16[16,32,2048]{2,1,0:T(8,128)(2,1)}), bf16[16,32,2048]{2,1,0:T(8,128)(2,1)S(1)}, u32[]{:S(2)}, u32[]{:S(2)}) async-start(bf16[16,32,2048]{2,1,0:T(8,128)(2,1)} %get-tuple-element.14), calls=%async_computation | async-start | bytes 4194304 | tf_op jit(solution)/shard_map/all_to_all | solution.py:223
  21.4 35.5 %all-gather = bf16[2048,128]{1,0:T(8,128)(2,1)S(1)} all-gather(bf16[64,128]{1,0:T(8,128)(2,1)S(1)} %reduce_sum.9), channel_id=2, replica_groups={{0,1,8,9,16,17,24,25,32,33,40,41,48,49,56,57,64,65,72,73,80,81,88,89,96..., dimensions={0}, use_global_device_ids=true | all-gather | bytes 540672 | tf_op jit(solution)/shard_map/all_gather | solution.py:227
  56.9 0.0 all-to-all-done
  57.0 0.7 shard_map.93
  57.7 14.5 %all_to_all.15.part_ref = f32[16,32,128]{2,1,0:T(8,128)S(1)} all-to-all(f32[16,32,128]{2,1,0:T(8,128)S(1)} %bitcast.14), channel_id=1, replica_groups={{0,2,4,6,128,130,132,134,256,258,260,262,384,386,388,390},{1,3,5,7,129,..., dimensions={0} | all-to-all | bytes 524288 | tf_op jit(solution)/shard_map/all_to_all | solution.py:232
  72.2 0.0 copy-done
  72.2 0.0 copy-done.1
  72.2 0.7 shard_map.94
  (1 shorter events, 0.0 us)
Async XLA Ops:
  2.1 15.5 %all-to-all-start.1 = ((bf16[8,64,128]{2,1,0:T(8,128)(2,1)}), bf16[8,64,128]{2,1,0:T(8,128)(2,1)S(1)}, u32[]{:S(2)}, u32[]{:S(2)}) async-start(bf16[8,64,128]{2,1,0:T(8,128)(2,1)} %bitcast.15), calls=%async_computation.1 | async-start | bytes 262144 | tf_op jit(solution)/shard_map/all_to_all | solution.py:205
  17.5 54.6 %copy-start = (f32[25,400]{1,0:T(8,128)S(1)}, f32[25,400]{1,0:T(8,128)}, u32[]{:S(2)}) copy-start(f32[25,400]{1,0:T(8,128)} %get-tuple-element.12.energy_ref) | copy-start | bytes 120004
  17.5 54.6 %copy-start.1 = (f32[25,400]{1,0:T(8,128)S(1)}, f32[25,400]{1,0:T(8,128)}, u32[]{:S(2)}) copy-start(f32[25,400]{1,0:T(8,128)} %get-tuple-element.13.same_ref) | copy-start | bytes 120004
  17.5 39.4 %all-to-all-start = ((bf16[16,32,2048]{2,1,0:T(8,128)(2,1)}), bf16[16,32,2048]{2,1,0:T(8,128)(2,1)S(1)}, u32[]{:S(2)}, u32[]{:S(2)}) async-start(bf16[16,32,2048]{2,1,0:T(8,128)(2,1)} %get-tuple-element.14), calls=%async_computation | async-start | bytes 4194304 | tf_op jit(solution)/shard_map/all_to_all | solution.py:223

commit v5 on v4

--- a/solution.py
+++ b/solution.py
@@ -16,6 +16,7 @@
 CHUNK = 4 * GROUP
 CHUNKS = 16
 PER_X = 4
+EARLY = CHUNKS // 2 * CHUNK
 WINDOW = 896
 F32, BF16, I32 = jnp.float32, jnp.bfloat16, jnp.int32
 HBM = pl.BlockSpec(memory_space=pltpu.HBM)
@@ -78,10 +79,12 @@
     return jnp.broadcast_to(wide, (8, 128))
 
 
-def head_kernel(b_hbm, c_hbm, occ_hbm, w_hbm, t_hbm, out_hbm, t_ref, b_irrep, c_irrep, occ, w_ref, out_ref, sems, t_sem, out_sem):
+def head_kernel(
+    b_hbm, c_hbm, occ_hbm, w_hbm, t_hbm, out_hbm, t_ref, b_irrep, c_irrep, occ, w_ref, out_ref, sems, t_sem, out_sem
+):
     copies = fetch((b_hbm, c_hbm, occ_hbm, w_hbm), (b_irrep, c_irrep, occ, w_ref), sems)
-    whole_t = pltpu.make_async_copy(t_hbm, t_ref, t_sem)
-    whole_t.start()
+    early = pltpu.make_async_copy(t_hbm.at[:, pl.ds(0, EARLY)], t_ref, t_sem)
+    early.start()
     out_ref[...] = jnp.zeros_like(out_ref)
     s = iota((COLS, 1), 0)
     hit = iota((COLS, O), 1) == mod_o(s)
@@ -96,12 +99,12 @@
     send = pltpu.make_async_copy(out_ref, out_hbm, out_sem)
     send.start()
     send.wait()
-    whole_t.wait()
+    early.wait()
 
 
 def t_kernel(
-    a_hbm, c_hbm, occ_hbm, b_hbm, ea_hbm, eb_hbm, eo_hbm, t_ref, out_hbm, energy, same,
-    a_irrep, c_lanes, occ, b_irrep, eps_a, eps_b, eps_occ, want, have, pick, kept, packed, sems, o_sems,
+    a_hbm, c_hbm, occ_hbm, b_hbm, ea_hbm, eb_hbm, eo_hbm, early, t_hbm, out_hbm, energy, same,
+    a_irrep, c_lanes, occ, b_irrep, eps_a, eps_b, eps_occ, late, want, have, pick, kept, packed, sems, t_sem, o_sems,
 ):
     def send(x, y):
         return pltpu.make_async_copy(packed.at[x], out_hbm.at[YS * x + y], o_sems.at[YS * x + y])
@@ -111,6 +114,8 @@
         (a_irrep, c_lanes, occ, b_irrep, eps_a, eps_b, eps_occ),
         sems,
     )
+    rest = pltpu.make_async_copy(t_hbm.at[:, pl.ds(EARLY, EARLY)], late, t_sem)
+    rest.start()
     at = iota((WINDOW + 96, 1), 0) - 96
     k = jnp.where((at >= 0) & (at < GROUP), mod_o(jnp.maximum(at, 0)), -1)
     pick[...] = jnp.where(k == iota((WINDOW + 96, KP), 1), 1.0, 0.0).astype(BF16)
@@ -120,7 +125,7 @@
     mod = mod_o(lane)
     over = (lane - mod) // O
     group = iota((8, 128), 0) // 4
-    for copy in copies:
+    for copy in copies[:3]:
         copy.wait()
     here = place()
     a, first = here // 4, ROWS * (here % 4)
@@ -132,10 +137,13 @@
         source = jnp.where(group == 0, lanes[0], lanes[1])
         have[8 * half : 8 * half + 8, :] = lookup(source, 32 * (iota((8, CHUNK), 0) % 4) + over).astype(F32)
     for x in range(XS):
+        if x == XS // 2:
+            rest.wait()
+        source, skip = (early, 0) if x < XS // 2 else (late, EARLY)
         part = slice(RP * PER_X * x, RP * PER_X * (x + 1))
         for q in range(PER_X * x, PER_X * (x + 1)):
             mask = want[:ROWS, :] == have[q : q + 1, :].astype(BF16)
-            got = t_ref[:, CHUNK * q : CHUNK * (q + 1)]
+            got = source[:, CHUNK * q - skip : CHUNK * (q + 1) - skip]
             kept[RP * q : RP * q + ROWS, :] = jnp.where(mask, got, jnp.zeros((), BF16))
         for j in range(4):
             full = jnp.dot(
@@ -148,6 +156,8 @@
                 packed[x, :, lanes] = full[RP * h : RP * (h + 1)].astype(BF16)
         for y in range(YS):
             send(x, y).start()
+    for copy in copies[3:]:
+        copy.wait()
     wide = 4 * NP
     col = (by_slab(b_irrep, I32) ^ occ_t[:, :wide])[:1, :COLS]
     column_energy = (by_slab(eps_b, F32) - lookup(padded(eps_occ[...]), mod[:, :wide]))[:1, :COLS]
@@ -193,7 +203,7 @@
     a_row, b_row, c_row, occ, eo = (lanes(v) for v in (a_irrep, b_irrep, c_irrep, occ_irrep, eps_occ))
     w_parts, t_near = call(
         head_kernel,
-        [pltpu.HBM((4 * NP, KP), BF16), vmem((ROWS, CHUNKS * CHUNK), BF16)],
+        [pltpu.HBM((4 * NP, KP), BF16), vmem((ROWS, EARLY), BF16)],
         10**7, 10**6, 56,
         in_specs=[HBM] * 5,
         out_specs=[HBM, whole],
@@ -206,19 +216,19 @@
     w_own = jnp.sum(w_got, axis=0, dtype=BF16)
     t_parts, energy, same = call(
         t_kernel,
-        [pltpu.HBM((XS * YS, RP, ZS * KP), BF16), struct((ROWS, COLS), F32), struct((ROWS, COLS), F32)],
+        [pltpu.HBM((XS * YS, RP, ZS * KP), BF16), vmem((ROWS, COLS), F32), vmem((ROWS, COLS), F32)],
         4 * 10**9, 4 * 10**6, 55,
-        in_specs=[HBM] * 7 + [whole],
+        in_specs=[HBM] * 7 + [whole, HBM],
         out_specs=[HBM, whole, whole],
         scratch_shapes=[
             smem((1, 128), I32), vmem((1, 512), I32), vmem((1, O), I32), smem((1, 4), I32), smem((1, 128), F32),
-            smem((1, 4), F32), vmem((1, O), F32), vmem((RP, CHUNK), BF16), vmem((CHUNKS, CHUNK), F32),
+            smem((1, 4), F32), vmem((1, O), F32), vmem((ROWS, EARLY), BF16), vmem((RP, CHUNK), BF16), vmem((CHUNKS, CHUNK), F32),
             vmem((WINDOW + 96, KP), BF16), vmem((CHUNKS * RP, CHUNK), BF16), vmem((XS, RP, ZS * KP), BF16),
-            dma((7,)), dma((XS * YS,)),
+            dma((7,)), dma, dma((XS * YS,)),
         ],
     )(
         a_row, c_row, occ, b_row, lanes(eps_a), lanes(eps_b), eo,
-        pltpu.with_memory_space_constraint(t_near, pltpu.VMEM),
+        pltpu.with_memory_space_constraint(t_near, pltpu.VMEM), t_slab,
     )
     t_got = lax.all_to_all(
         t_parts, ("idx", "rep"), split_axis=0, concat_axis=0, axis_index_groups=CORE_PLANES, tiled=True
@@ -235,7 +245,7 @@
     )
     return call(
         end_kernel, struct((ROWS, COLS), F32), 10**6, 10**6, 24, in_specs=[whole] * 3, out_specs=whole
-    )(energy, same, ends)
+    )(*(pltpu.with_memory_space_constraint(near, pltpu.VMEM) for near in (energy, same)), ends)
 
 
 def solution(mesh):

time: 73.2 us -> 72.6 us (level)
  Pallas kernels: 7.22 us -> 6.36 us
    pallas_call x2, Pallas kernels: 5.86 us -> 5 us  [the longest x1 3.25 us: per_device(): call(t_kernel, [pltpu.HBM((XS * YS, RP, ZS * KP), BF16), vmem((ROWS, COLS...]
  transfers between devices with their start and end apart: 2 -> 2, of which waited for: 1 -> 1; matrix products, arithmetic and copies ran while one was open for 0% -> 0% of each run, Pallas kernels for 5% -> 4%
where the time goes in v5:
time: 72.6 us; the launch traced here: 72.3 us
  blocking collectives  50 us (69%)
  starting transfers between devices  13.9 us (19%)
  Pallas kernels  6.36 us (9%)
  waiting for transfers between devices  2.04 us (3%)
    all_gather x1, blocking collectives, per_device(): lax.all_gather(w_own, ('idx', 'rep'), axis=0, axis_index_groups=Z_CORE_GR...  35.5 us
    all_to_all x1, blocking collectives, per_device(): lax.all_to_all(partial.reshape(-1, RP, NP), ('idx', 'rep'), split_axis=0,...  14.5 us
    all_to_all x1, starting transfers between devices, per_device(): lax.all_to_all(w_parts.reshape(8, NP // 2, KP), 'rep', split_axis=0, conc...  10.2 us
    all_to_all x1, starting transfers between devices, per_device(): lax.all_to_all(t_parts, ('idx', 'rep'), split_axis=0, concat_axis=0, axis...  3.72 us
    pallas_call x1, Pallas kernels, per_device(): call(t_kernel, [pltpu.HBM((XS * YS, RP, ZS * KP), BF16), vmem((ROWS, COLS...  3.25 us
    all_to_all x1, waiting for transfers between devices, per_device(): lax.all_to_all(w_parts.reshape(8, NP // 2, KP), 'rep', split_axis=0, conc...  2.04 us
    pallas_call x1, Pallas kernels, per_device(): call(head_kernel, [pltpu.HBM((4 * NP, KP), BF16), vmem((ROWS, EARLY), BF1...  1.75 us
  transfers between devices with their start and end apart: 2, of which 1 were waited for; matrix products, arithmetic and copies ran while one was open for 0% of the time, Pallas kernels for 4%

profile of v5, /device:TPU:1, one launch (start us, length us, event | category | flops | bytes accessed | tf_op | source)
XLA Modules:
  0.0 72.3 jit_solution(6542227433812676591)
XLA Ops:
  0.0 1.7 %shard_map.91 = (bf16[512,128]{1,0:T(8,128)(2,1)}, bf16[25,25600]{1,0:T(8,128)(2,1)S(1)}) custom-call(s32[1,4]{1,0:T(1,128)} %bitcast.21, s32[1,512]{1,0:T(1,128)} %bitcast.17, s32[1,100]{1,0:T(1,128)} %bitcast.19, bf16[400,100]{1,0:T(8,128)(2,1)} %bitcast.16, bf16[25,51200]{1,0:T(8,128)(2,1)} %t_hbm.3), custom_call_target="tpu_custom_call" | custom-call | flops 10000000 | bytes 1000000 | tf_op jit(solution)/shard_map/pallas_call | solution.py:204
  1.8 10.2 %all-to-all-start.1 = ((bf16[8,64,128]{2,1,0:T(8,128)(2,1)}), bf16[8,64,128]{2,1,0:T(8,128)(2,1)S(1)}, u32[]{:S(2)}, u32[]{:S(2)}) async-start(bf16[8,64,128]{2,1,0:T(8,128)(2,1)} %bitcast.15), calls=%async_computation.1 | async-start | bytes 262144 | tf_op jit(solution)/shard_map/all_to_all | solution.py:215
  11.9 3.2 %shard_map.92 = (bf16[16,32,2048]{2,1,0:T(8,128)(2,1)}, f32[25,400]{1,0:T(8,128)S(1)}, f32[25,400]{1,0:T(8,128)S(1)}) custom-call(s32[1,128]{1,0:T(1,128)} %bitcast.23, s32[1,512]{1,0:T(1,128)} %bitcast.18, s32[1,100]{1,0:T(1,128)} %bitcast.20, s32[1,4]{1,0:T(1,128)} %bitcast.22, f32[1,128]{1,0:T(1,128)} %bitcast.24, f32[1,4]{1,0:T(1,128)} %bitcast.25, ...), custom_call_target="tpu_custom_call" | custom-call | flops 4000000000 | bytes 4000000 | tf_op jit(solution)/shard_map/pallas_call | solution.py:217
  15.2 2.0 %all-to-all-done.1 = bf16[8,64,128]{2,1,0:T(8,128)(2,1)S(1)} async-done(((bf16[8,64,128]{2,1,0:T(8,128)(2,1)}), bf16[8,64,128]{2,1,0:T(8,128)(2,1)S(1)}, u32[]{:S(2)}, u32[]{:S(2)}) %all-to-all-start.1) | async-done | bytes 131104 | tf_op jit(solution)/shard_map/all_to_all | solution.py:215
  17.2 3.7 %all-to-all-start = ((bf16[16,32,2048]{2,1,0:T(8,128)(2,1)}), bf16[16,32,2048]{2,1,0:T(8,128)(2,1)S(1)}, u32[]{:S(2)}, u32[]{:S(2)}) async-start(bf16[16,32,2048]{2,1,0:T(8,128)(2,1)} %get-tuple-element.14), calls=%async_computation | async-start | bytes 4194304 | tf_op jit(solution)/shard_map/all_to_all | solution.py:233
  21.0 35.5 %all-gather = bf16[2048,128]{1,0:T(8,128)(2,1)S(1)} all-gather(bf16[64,128]{1,0:T(8,128)(2,1)S(1)} %reduce_sum.9), channel_id=2, replica_groups={{0,1,8,9,16,17,24,25,32,33,40,41,48,49,56,57,64,65,72,73,80,81,88,89,96..., dimensions={0}, use_global_device_ids=true | all-gather | bytes 540672 | tf_op jit(solution)/shard_map/all_gather | solution.py:237
  56.4 0.0 all-to-all-done
  56.4 0.7 shard_map.93
  57.1 14.5 %all_to_all.15.part_ref = f32[16,32,128]{2,1,0:T(8,128)S(1)} all-to-all(f32[16,32,128]{2,1,0:T(8,128)S(1)} %bitcast.14), channel_id=1, replica_groups={{0,2,4,6,128,130,132,134,256,258,260,262,384,386,388,390},{1,3,5,7,129,..., dimensions={0} | all-to-all | bytes 524288 | tf_op jit(solution)/shard_map/all_to_all | solution.py:242
  71.7 0.7 shard_map.94
  (1 shorter events, 0.0 us)
Async XLA Ops:
  1.8 15.5 %all-to-all-start.1 = ((bf16[8,64,128]{2,1,0:T(8,128)(2,1)}), bf16[8,64,128]{2,1,0:T(8,128)(2,1)S(1)}, u32[]{:S(2)}, u32[]{:S(2)}) async-start(bf16[8,64,128]{2,1,0:T(8,128)(2,1)} %bitcast.15), calls=%async_computation.1 | async-start | bytes 262144 | tf_op jit(solution)/shard_map/all_to_all | solution.py:215
  17.2 39.2 %all-to-all-start = ((bf16[16,32,2048]{2,1,0:T(8,128)(2,1)}), bf16[16,32,2048]{2,1,0:T(8,128)(2,1)S(1)}, u32[]{:S(2)}, u32[]{:S(2)}) async-start(bf16[16,32,2048]{2,1,0:T(8,128)(2,1)} %get-tuple-element.14), calls=%async_computation | async-start | bytes 4194304 | tf_op jit(solution)/shard_map/all_to_all | solution.py:233

commit v6 on v5

--- a/solution.py
+++ b/solution.py
@@ -8,6 +8,8 @@
 O = 100
 G = 8
 COLS = 400
+SLABS = 4
+SP = 112
 NP = 128
 KP = 128
 RP = 32
@@ -22,9 +24,10 @@
 HBM = pl.BlockSpec(memory_space=pltpu.HBM)
 ZS, XS, YS, CS = 16, 4, 4, 2
 Z_GROUPS = [[x * ZS + z for z in range(ZS)] for x in range(XS)]
-CORE_PLANES = [
-    [(x * ZS + z) * YS * CS + y * CS + c for x in range(XS) for y in range(YS)]
+WORK_GROUPS = [
+    [(x * ZS + z) * YS * CS + (2 * high + low) * CS + c for x in range(XS) for low in range(2)]
     for z in range(ZS)
+    for high in range(2)
     for c in range(CS)
 ]
 Z_CORE_GROUPS = [
@@ -55,14 +58,6 @@
     return jnp.concatenate(parts, axis=1)
 
 
-def by_slab(ref, dtype):
-    s = iota((8, 4 * NP), 1)
-    out = jnp.full((8, 4 * NP), ref[0, 0], dtype)
-    for b in range(1, COLS // O):
-        out = jnp.where(s >= b * O, ref[0, b], out)
-    return out
-
-
 def fetch(sources, targets, sems):
     copies = [pltpu.make_async_copy(s, t, sems.at[i]) for i, (s, t) in enumerate(zip(sources, targets))]
     for copy in copies:
@@ -86,16 +81,16 @@
     early = pltpu.make_async_copy(t_hbm.at[:, pl.ds(0, EARLY)], t_ref, t_sem)
     early.start()
     out_ref[...] = jnp.zeros_like(out_ref)
-    s = iota((COLS, 1), 0)
-    hit = iota((COLS, O), 1) == mod_o(s)
     for copy in copies:
         copy.wait()
-    slab = jnp.full((COLS, 1), b_irrep[0, 0], I32)
-    for b in range(1, COLS // O):
-        slab = jnp.where(s >= b * O, b_irrep[0, b], slab)
-    col = slab ^ jnp.sum(jnp.where(hit, occ[...].astype(F32), 0.0), axis=1, keepdims=True).astype(I32)
+    column = to_rows(occ[...].astype(F32), O, 0).astype(I32)
     row = c_irrep[0, place()] ^ occ[...]
-    out_ref[:COLS, :O] = jnp.where(row == col, w_ref[...].astype(F32), 0.0).astype(BF16)
+    same = column ^ row
+    w = w_ref[...].astype(F32)
+    for b in range(SLABS):
+        kept = jnp.where(same == b_irrep[0, b], w[O * b : O * (b + 1)], 0.0).astype(BF16)
+        for high in range(2):
+            out_ref[SLABS * high + b, :O, :O] = kept
     send = pltpu.make_async_copy(out_ref, out_hbm, out_sem)
     send.start()
     send.wait()
@@ -107,7 +102,7 @@
     a_irrep, c_lanes, occ, b_irrep, eps_a, eps_b, eps_occ, late, want, have, pick, kept, packed, sems, t_sem, o_sems,
 ):
     def send(x, y):
-        return pltpu.make_async_copy(packed.at[x], out_hbm.at[YS * x + y], o_sems.at[YS * x + y])
+        return pltpu.make_async_copy(packed.at[x], out_hbm.at[2 * x + y], o_sems.at[2 * x + y])
 
     copies = fetch(
         (a_hbm, c_hbm, occ_hbm, b_hbm, ea_hbm, eb_hbm, eo_hbm),
@@ -154,35 +149,36 @@
             for h in range(PER_X):
                 lanes = slice(KP * (4 * h + j), KP * (4 * h + j + 1))
                 packed[x, :, lanes] = full[RP * h : RP * (h + 1)].astype(BF16)
-        for y in range(YS):
+        for y in range(2):
             send(x, y).start()
     for copy in copies[3:]:
         copy.wait()
-    wide = 4 * NP
-    col = (by_slab(b_irrep, I32) ^ occ_t[:, :wide])[:1, :COLS]
-    column_energy = (by_slab(eps_b, F32) - lookup(padded(eps_occ[...]), mod[:, :wide]))[:1, :COLS]
-    energy[...] = (eps_a[0, a] - to_rows(eps_occ[...], ROWS, first)) + column_energy
-    same[...] = jnp.where(row[:ROWS] == col, 1.0, 0.0)
+    row_energy = eps_a[0, a] - to_rows(eps_occ[...], ROWS, first)
+    for b in range(SLABS):
+        energy[b] = row_energy + (eps_b[0, b] - eps_occ[...])
+        same[b] = jnp.where(row[:ROWS] == (b_irrep[0, b] ^ occ[...]), 1.0, 0.0)
     for x in range(XS):
-        for y in range(YS):
+        for y in range(2):
             send(x, y).wait()
 
 
 def mm_kernel(t_ref, w_ref, out_ref):
-    w_t = jnp.concatenate([w_ref[z] for z in range(ZS)], axis=1)
-    out_ref[...] = lax.dot_general(
-        t_ref[...], w_t, (((1,), (1,)), ((), ())), preferred_element_type=F32
-    )
+    out_ref[...] = jnp.zeros_like(out_ref)
+    for c in range(CS):
+        w_t = jnp.concatenate([w_ref[CS * z + c] for z in range(ZS)], axis=1)
+        got = lax.dot_general(t_ref[...], w_t, (((1,), (1,)), ((), ())), preferred_element_type=F32)
+        out_ref[:, NP * c : NP * c + SP] = got
 
 
 def end_kernel(energy_ref, same_ref, part_ref, out_ref):
-    for n in range(4):
-        lo, hi = NP * n, min(NP * n + NP, COLS)
-        total = part_ref[n, :ROWS, : hi - lo]
+    for b in range(SLABS):
+        low, c = divmod(b, CS)
+        lanes = slice(NP * c, NP * c + O)
+        total = part_ref[low, :ROWS, lanes]
         for x in range(1, XS):
-            total = total + part_ref[YS * x + n, :ROWS, : hi - lo]
-        total = jnp.where(same_ref[:, lo:hi] > 0.5, total, 0.0)
-        out_ref[:, lo:hi] = total / energy_ref[:, lo:hi]
+            total = total + part_ref[2 * x + low, :ROWS, lanes]
+        total = jnp.where(same_ref[b] > 0.5, total, 0.0)
+        out_ref[:, O * b : O * (b + 1)] = total / energy_ref[b]
 
 
 def call(kernel, out, flops, moved, room, **rest):
@@ -203,20 +199,20 @@
     a_row, b_row, c_row, occ, eo = (lanes(v) for v in (a_irrep, b_irrep, c_irrep, occ_irrep, eps_occ))
     w_parts, t_near = call(
         head_kernel,
-        [pltpu.HBM((4 * NP, KP), BF16), vmem((ROWS, EARLY), BF16)],
+        [pltpu.HBM((2 * SLABS, SP, KP), BF16), vmem((ROWS, EARLY), BF16)],
         10**7, 10**6, 56,
         in_specs=[HBM] * 5,
         out_specs=[HBM, whole],
         scratch_shapes=[
             smem((1, 4), I32), smem((1, 512), I32), vmem((1, O), I32), vmem((COLS, O), BF16),
-            vmem((4 * NP, KP), BF16), dma((4,)), dma, dma,
+            vmem((2 * SLABS, SP, KP), BF16), dma((4,)), dma, dma,
         ],
     )(b_row, c_row, occ, w_cycle.T, t_slab)
-    w_got = lax.all_to_all(w_parts.reshape(8, NP // 2, KP), "rep", split_axis=0, concat_axis=0, tiled=True)
+    w_got = lax.all_to_all(w_parts, "rep", split_axis=0, concat_axis=0, tiled=True)
     w_own = jnp.sum(w_got, axis=0, dtype=BF16)
     t_parts, energy, same = call(
         t_kernel,
-        [pltpu.HBM((XS * YS, RP, ZS * KP), BF16), vmem((ROWS, COLS), F32), vmem((ROWS, COLS), F32)],
+        [pltpu.HBM((2 * XS, RP, ZS * KP), BF16), vmem((SLABS, ROWS, O), F32), vmem((SLABS, ROWS, O), F32)],
         4 * 10**9, 4 * 10**6, 55,
         in_specs=[HBM] * 7 + [whole, HBM],
         out_specs=[HBM, whole, whole],
@@ -224,24 +220,24 @@
             smem((1, 128), I32), vmem((1, 512), I32), vmem((1, O), I32), smem((1, 4), I32), smem((1, 128), F32),
             smem((1, 4), F32), vmem((1, O), F32), vmem((ROWS, EARLY), BF16), vmem((RP, CHUNK), BF16), vmem((CHUNKS, CHUNK), F32),
             vmem((WINDOW + 96, KP), BF16), vmem((CHUNKS * RP, CHUNK), BF16), vmem((XS, RP, ZS * KP), BF16),
-            dma((7,)), dma, dma((XS * YS,)),
+            dma((7,)), dma, dma((2 * XS,)),
         ],
     )(
         a_row, c_row, occ, b_row, lanes(eps_a), lanes(eps_b), eo,
         pltpu.with_memory_space_constraint(t_near, pltpu.VMEM), t_slab,
     )
     t_got = lax.all_to_all(
-        t_parts, ("idx", "rep"), split_axis=0, concat_axis=0, axis_index_groups=CORE_PLANES, tiled=True
+        t_parts, ("idx", "rep"), split_axis=0, concat_axis=0, axis_index_groups=WORK_GROUPS, tiled=True
     )
     w_own, t_parts = lax.optimization_barrier((w_own, t_parts))
     w_z = lax.all_gather(w_own, ("idx", "rep"), axis=0, axis_index_groups=Z_CORE_GROUPS)
     partial = call(
-        mm_kernel, struct((XS * YS * RP, NP), F32), 2 * 512 * 2048 * 128, 3 * 10**6, 24,
+        mm_kernel, struct((2 * XS * RP, CS * NP), F32), 2 * 512 * 2048 * 128, 3 * 10**6, 24,
         in_specs=[whole] * 2, out_specs=whole,
-    )(t_got.reshape(-1, ZS * KP), w_z.reshape(ZS, NP, KP))
+    )(t_got.reshape(-1, ZS * KP), w_z)
     ends = lax.all_to_all(
-        partial.reshape(-1, RP, NP), ("idx", "rep"), split_axis=0, concat_axis=0,
-        axis_index_groups=CORE_PLANES, tiled=True,
+        partial.reshape(2 * XS, RP, CS * NP), ("idx", "rep"), split_axis=0, concat_axis=0,
+        axis_index_groups=WORK_GROUPS, tiled=True,
     )
     return call(
         end_kernel, struct((ROWS, COLS), F32), 10**6, 10**6, 24, in_specs=[whole] * 3, out_specs=whole

time: 72.6 us -> 71.2 us (0.981)
  blocking collectives: 50 us -> 47.6 us
  waiting for transfers between devices: 2.04 us -> 3.13 us
    all_to_all x1, blocking collectives: 14.5 us -> 11.5 us  [per_device(): lax.all_to_all(partial.reshape(2 * XS, RP, CS * NP), ('idx', 'rep'), spli...]
    all_to_all x1, waiting for transfers between devices: 2.04 us -> 3.13 us  [per_device(): lax.all_to_all(w_parts, 'rep', split_axis=0, concat_axis=0, tiled=True)]
where the time goes in v6:
time: 71.2 us; the launch traced here: 70.8 us
  blocking collectives  47.6 us (67%)
  starting transfers between devices  13.8 us (19%)
  Pallas kernels  6.26 us (9%)
  waiting for transfers between devices  3.13 us (4%)
    all_gather x1, blocking collectives, per_device(): lax.all_gather(w_own, ('idx', 'rep'), axis=0, axis_index_groups=Z_CORE_GR...  36.1 us
    all_to_all x1, blocking collectives, per_device(): lax.all_to_all(partial.reshape(2 * XS, RP, CS * NP), ('idx', 'rep'), spli...  11.5 us
    all_to_all x1, starting transfers between devices, per_device(): lax.all_to_all(w_parts, 'rep', split_axis=0, concat_axis=0, tiled=True)  10.2 us
    all_to_all x1, starting transfers between devices, per_device(): lax.all_to_all(t_parts, ('idx', 'rep'), split_axis=0, concat_axis=0, axis...  3.56 us
    all_to_all x1, waiting for transfers between devices, per_device(): lax.all_to_all(w_parts, 'rep', split_axis=0, concat_axis=0, tiled=True)  3.13 us
    pallas_call x1, Pallas kernels, per_device(): call(t_kernel, [pltpu.HBM((2 * XS, RP, ZS * KP), BF16), vmem((SLABS, ROWS...  3.08 us
    pallas_call x1, Pallas kernels, per_device(): call(head_kernel, [pltpu.HBM((2 * SLABS, SP, KP), BF16), vmem((ROWS, EARL...  1.78 us
  transfers between devices with their start and end apart: 2, of which 1 were waited for; matrix products, arithmetic and copies ran while one was open for 0% of the time, Pallas kernels for 4%

profile of v6, /device:TPU:1, one launch (start us, length us, event | category | flops | bytes accessed | tf_op | source)
XLA Modules:
  0.0 70.8 jit_solution(8463639934909800096)
XLA Ops:
  0.0 1.8 %shard_map.91 = (bf16[8,112,128]{2,1,0:T(8,128)(2,1)}, bf16[25,25600]{1,0:T(8,128)(2,1)S(1)}) custom-call(s32[1,4]{1,0:T(1,128)} %bitcast.19, s32[1,512]{1,0:T(1,128)} %bitcast.15, s32[1,100]{1,0:T(1,128)} %bitcast.17, bf16[400,100]{1,0:T(8,128)(2,1)} %bitcast.14, bf16[25,51200]{1,0:T(8,128)(2,1)} %t_hbm.3), custom_call_target="tpu_custom_call" | custom-call | flops 10000000 | bytes 1000000 | tf_op jit(solution)/shard_map/pallas_call | solution.py:200
  1.8 10.2 %all-to-all-start.1 = ((bf16[8,112,128]{2,1,0:T(8,128)(2,1)}), bf16[8,112,128]{2,1,0:T(8,128)(2,1)S(1)}, u32[]{:S(2)}, u32[]{:S(2)}) async-start(bf16[8,112,128]{2,1,0:T(8,128)(2,1)} %get-tuple-element.15), calls=%async_computation.1 | async-start | bytes 458752 | tf_op jit(solution)/shard_map/all_to_all | solution.py:211
  12.0 3.1 %shard_map.92 = (bf16[8,32,2048]{2,1,0:T(8,128)(2,1)}, f32[4,25,100]{2,1,0:T(8,128)S(1)}, f32[4,25,100]{2,1,0:T(8,128)S(1)}) custom-call(s32[1,128]{1,0:T(1,128)} %bitcast.21, s32[1,512]{1,0:T(1,128)} %bitcast.16, s32[1,100]{1,0:T(1,128)} %bitcast.18, s32[1,4]{1,0:T(1,128)} %bitcast.20, f32[1,128]{1,0:T(1,128)} %bitcast.22, f32[1,4]{1,0:T(1,128)} %bitcast.23, ...), custom_call_target="tpu_custom_call" | custom-call | flops 4000000000 | bytes 4000000 | tf_op jit(solution)/shard_map/pallas_call | solution.py:213
  15.1 3.1 %all-to-all-done.1 = bf16[8,112,128]{2,1,0:T(8,128)(2,1)S(1)} async-done(((bf16[8,112,128]{2,1,0:T(8,128)(2,1)}), bf16[8,112,128]{2,1,0:T(8,128)(2,1)S(1)}, u32[]{:S(2)}, u32[]{:S(2)}) %all-to-all-start.1) | async-done | bytes 229408 | tf_op jit(solution)/shard_map/all_to_all | solution.py:211
  18.2 3.6 %all-to-all-start = ((bf16[8,32,2048]{2,1,0:T(8,128)(2,1)}), bf16[8,32,2048]{2,1,0:T(8,128)(2,1)S(1)}, u32[]{:S(2)}, u32[]{:S(2)}) async-start(bf16[8,32,2048]{2,1,0:T(8,128)(2,1)} %get-tuple-element.14), calls=%async_computation | async-start | bytes 2097152 | tf_op jit(solution)/shard_map/all_to_all | solution.py:229
  21.8 36.1 %all-gather = bf16[3584,128]{1,0:T(8,128)(2,1)S(1)} all-gather(bf16[112,128]{1,0:T(8,128)(2,1)S(1)} %reduce_sum.9), channel_id=2, replica_groups={{0,1,8,9,16,17,24,25,32,33,40,41,48,49,56,57,64,65,72,73,80,81,88,89,96..., dimensions={0}, use_global_device_ids=true | all-gather | bytes 946176 | tf_op jit(solution)/shard_map/all_gather | solution.py:233
  57.9 0.0 all-to-all-done
  57.9 0.7 shard_map.93
  58.6 11.5 %all_to_all.15.part_ref = f32[8,32,256]{2,1,0:T(8,128)S(1)} all-to-all(f32[8,32,256]{2,1,0:T(8,128)S(1)} %bitcast.13), channel_id=1, replica_groups={{0,2,128,130,256,258,384,386},{1,3,129,131,257,259,385,387},{4,6,132,13..., dimensions={0} | all-to-all | bytes 524288 | tf_op jit(solution)/shard_map/all_to_all | solution.py:238
  70.1 0.7 %shard_map.94 = f32[25,400]{1,0:T(8,128)} custom-call(f32[4,25,100]{2,1,0:T(8,128)S(1)} %get-tuple-element.12.energy_ref, f32[4,25,100]{2,1,0:T(8,128)S(1)} %get-tuple-element.13.same_ref, f32[8,32,256]{2,1,0:T(8,128)S(1)} %all_to_all.15.part_ref), custom_call_target="tpu_custom_call" | custom-call | flops 1000000 | bytes 1000000 | tf_op jit(solution)/shard_map/pallas_call | solution.py:242
  (1 shorter events, 0.0 us)
Async XLA Ops:
  1.8 16.4 %all-to-all-start.1 = ((bf16[8,112,128]{2,1,0:T(8,128)(2,1)}), bf16[8,112,128]{2,1,0:T(8,128)(2,1)S(1)}, u32[]{:S(2)}, u32[]{:S(2)}) async-start(bf16[8,112,128]{2,1,0:T(8,128)(2,1)} %get-tuple-element.15), calls=%async_computation.1 | async-start | bytes 458752 | tf_op jit(solution)/shard_map/all_to_all | solution.py:211
  18.2 39.7 %all-to-all-start = ((bf16[8,32,2048]{2,1,0:T(8,128)(2,1)}), bf16[8,32,2048]{2,1,0:T(8,128)(2,1)S(1)}, u32[]{:S(2)}, u32[]{:S(2)}) async-start(bf16[8,32,2048]{2,1,0:T(8,128)(2,1)} %get-tuple-element.14), calls=%async_computation | async-start | bytes 2097152 | tf_op jit(solution)/shard_map/all_to_all | solution.py:229

commit v7 on v6

--- a/solution.py
+++ b/solution.py
@@ -89,11 +89,15 @@
     w = w_ref[...].astype(F32)
     for b in range(SLABS):
         kept = jnp.where(same == b_irrep[0, b], w[O * b : O * (b + 1)], 0.0).astype(BF16)
-        for high in range(2):
-            out_ref[SLABS * high + b, :O, :O] = kept
-    send = pltpu.make_async_copy(out_ref, out_hbm, out_sem)
-    send.start()
-    send.wait()
+        out_ref[b, :O, :O] = kept
+    sends = [
+        pltpu.make_async_copy(out_ref, out_hbm.at[pl.ds(SLABS * high, SLABS)], out_sem.at[high])
+        for high in range(2)
+    ]
+    for send in sends:
+        send.start()
+    for send in sends:
+        send.wait()
     early.wait()
 
 
@@ -163,11 +167,14 @@
 
 
 def mm_kernel(t_ref, w_ref, out_ref):
-    out_ref[...] = jnp.zeros_like(out_ref)
+    none = jnp.zeros((NP - SP, ZS * KP), BF16)
+    rows = []
     for c in range(CS):
-        w_t = jnp.concatenate([w_ref[CS * z + c] for z in range(ZS)], axis=1)
-        got = lax.dot_general(t_ref[...], w_t, (((1,), (1,)), ((), ())), preferred_element_type=F32)
-        out_ref[:, NP * c : NP * c + SP] = got
+        rows += [jnp.concatenate([w_ref[CS * z + c] for z in range(ZS)], axis=1), none]
+    w_t = jnp.concatenate(rows, axis=0)
+    out_ref[...] = lax.dot_general(
+        t_ref[...], w_t, (((1,), (1,)), ((), ())), preferred_element_type=F32
+    )
 
 
 def end_kernel(energy_ref, same_ref, part_ref, out_ref):
@@ -205,7 +212,7 @@
         out_specs=[HBM, whole],
         scratch_shapes=[
             smem((1, 4), I32), smem((1, 512), I32), vmem((1, O), I32), vmem((COLS, O), BF16),
-            vmem((2 * SLABS, SP, KP), BF16), dma((4,)), dma, dma,
+            vmem((SLABS, SP, KP), BF16), dma((4,)), dma, dma((2,)),
         ],
     )(b_row, c_row, occ, w_cycle.T, t_slab)
     w_got = lax.all_to_all(w_parts, "rep", split_axis=0, concat_axis=0, tiled=True)

time: 71.2 us -> 71 us (level)
  no operation moved by 1% of the time
where the time goes in v7:
time: 71 us; the launch traced here: 70.6 us
  blocking collectives  47.6 us (67%)
  starting transfers between devices  13.8 us (19%)
  Pallas kernels  6.04 us (9%)
  waiting for transfers between devices  3.13 us (4%)
    all_gather x1, blocking collectives, per_device(): lax.all_gather(w_own, ('idx', 'rep'), axis=0, axis_index_groups=Z_CORE_GR...  36.1 us
    all_to_all x1, blocking collectives, per_device(): lax.all_to_all(partial.reshape(2 * XS, RP, CS * NP), ('idx', 'rep'), spli...  11.6 us
    all_to_all x1, starting transfers between devices, per_device(): lax.all_to_all(w_parts, 'rep', split_axis=0, concat_axis=0, tiled=True)  10.2 us
    all_to_all x1, starting transfers between devices, per_device(): lax.all_to_all(t_parts, ('idx', 'rep'), split_axis=0, concat_axis=0, axis...  3.56 us
    all_to_all x1, waiting for transfers between devices, per_device(): lax.all_to_all(w_parts, 'rep', split_axis=0, concat_axis=0, tiled=True)  3.13 us
    pallas_call x1, Pallas kernels, per_device(): call(t_kernel, [pltpu.HBM((2 * XS, RP, ZS * KP), BF16), vmem((SLABS, ROWS...  3.08 us
    pallas_call x1, Pallas kernels, per_device(): call(head_kernel, [pltpu.HBM((2 * SLABS, SP, KP), BF16), vmem((ROWS, EARL...  1.78 us
  transfers between devices with their start and end apart: 2, of which 1 were waited for; matrix products, arithmetic and copies ran while one was open for 0% of the time, Pallas kernels for 4%

profile of v7, /device:TPU:1, one launch (start us, length us, event | category | flops | bytes accessed | tf_op | source)
XLA Modules:
  0.0 70.6 jit_solution(7189709743083980083)
XLA Ops:
  0.0 1.8 %shard_map.91 = (bf16[8,112,128]{2,1,0:T(8,128)(2,1)}, bf16[25,25600]{1,0:T(8,128)(2,1)S(1)}) custom-call(s32[1,4]{1,0:T(1,128)} %bitcast.19, s32[1,512]{1,0:T(1,128)} %bitcast.15, s32[1,100]{1,0:T(1,128)} %bitcast.17, bf16[400,100]{1,0:T(8,128)(2,1)} %bitcast.14, bf16[25,51200]{1,0:T(8,128)(2,1)} %t_hbm.3), custom_call_target="tpu_custom_call" | custom-call | flops 10000000 | bytes 1000000 | tf_op jit(solution)/shard_map/pallas_call | solution.py:207
  1.8 10.2 %all-to-all-start.1 = ((bf16[8,112,128]{2,1,0:T(8,128)(2,1)}), bf16[8,112,128]{2,1,0:T(8,128)(2,1)S(1)}, u32[]{:S(2)}, u32[]{:S(2)}) async-start(bf16[8,112,128]{2,1,0:T(8,128)(2,1)} %get-tuple-element.15), calls=%async_computation.1 | async-start | bytes 458752 | tf_op jit(solution)/shard_map/all_to_all | solution.py:218
  12.0 3.1 %shard_map.92 = (bf16[8,32,2048]{2,1,0:T(8,128)(2,1)}, f32[4,25,100]{2,1,0:T(8,128)S(1)}, f32[4,25,100]{2,1,0:T(8,128)S(1)}) custom-call(s32[1,128]{1,0:T(1,128)} %bitcast.21, s32[1,512]{1,0:T(1,128)} %bitcast.16, s32[1,100]{1,0:T(1,128)} %bitcast.18, s32[1,4]{1,0:T(1,128)} %bitcast.20, f32[1,128]{1,0:T(1,128)} %bitcast.22, f32[1,4]{1,0:T(1,128)} %bitcast.23, ...), custom_call_target="tpu_custom_call" | custom-call | flops 4000000000 | bytes 4000000 | tf_op jit(solution)/shard_map/pallas_call | solution.py:220
  15.1 3.1 %all-to-all-done.1 = bf16[8,112,128]{2,1,0:T(8,128)(2,1)S(1)} async-done(((bf16[8,112,128]{2,1,0:T(8,128)(2,1)}), bf16[8,112,128]{2,1,0:T(8,128)(2,1)S(1)}, u32[]{:S(2)}, u32[]{:S(2)}) %all-to-all-start.1) | async-done | bytes 229408 | tf_op jit(solution)/shard_map/all_to_all | solution.py:218
  18.2 3.6 %all-to-all-start = ((bf16[8,32,2048]{2,1,0:T(8,128)(2,1)}), bf16[8,32,2048]{2,1,0:T(8,128)(2,1)S(1)}, u32[]{:S(2)}, u32[]{:S(2)}) async-start(bf16[8,32,2048]{2,1,0:T(8,128)(2,1)} %get-tuple-element.14), calls=%async_computation | async-start | bytes 2097152 | tf_op jit(solution)/shard_map/all_to_all | solution.py:236
  21.8 36.1 %all-gather = bf16[3584,128]{1,0:T(8,128)(2,1)S(1)} all-gather(bf16[112,128]{1,0:T(8,128)(2,1)S(1)} %reduce_sum.9), channel_id=2, replica_groups={{0,1,8,9,16,17,24,25,32,33,40,41,48,49,56,57,64,65,72,73,80,81,88,89,96..., dimensions={0}, use_global_device_ids=true | all-gather | bytes 946176 | tf_op jit(solution)/shard_map/all_gather | solution.py:240
  57.9 0.0 all-to-all-done
  57.9 0.5 shard_map.93
  58.4 11.6 %all_to_all.15.part_ref = f32[8,32,256]{2,1,0:T(8,128)S(1)} all-to-all(f32[8,32,256]{2,1,0:T(8,128)S(1)} %bitcast.13), channel_id=1, replica_groups={{0,2,128,130,256,258,384,386},{1,3,129,131,257,259,385,387},{4,6,132,13..., dimensions={0} | all-to-all | bytes 524288 | tf_op jit(solution)/shard_map/all_to_all | solution.py:245
  69.9 0.7 %shard_map.94 = f32[25,400]{1,0:T(8,128)} custom-call(f32[4,25,100]{2,1,0:T(8,128)S(1)} %get-tuple-element.12.energy_ref, f32[4,25,100]{2,1,0:T(8,128)S(1)} %get-tuple-element.13.same_ref, f32[8,32,256]{2,1,0:T(8,128)S(1)} %all_to_all.15.part_ref), custom_call_target="tpu_custom_call" | custom-call | flops 1000000 | bytes 1000000 | tf_op jit(solution)/shard_map/pallas_call | solution.py:249
  (1 shorter events, 0.0 us)
Async XLA Ops:
  1.8 16.4 %all-to-all-start.1 = ((bf16[8,112,128]{2,1,0:T(8,128)(2,1)}), bf16[8,112,128]{2,1,0:T(8,128)(2,1)S(1)}, u32[]{:S(2)}, u32[]{:S(2)}) async-start(bf16[8,112,128]{2,1,0:T(8,128)(2,1)} %get-tuple-element.15), calls=%async_computation.1 | async-start | bytes 458752 | tf_op jit(solution)/shard_map/all_to_all | solution.py:218
  18.2 39.7 %all-to-all-start = ((bf16[8,32,2048]{2,1,0:T(8,128)(2,1)}), bf16[8,32,2048]{2,1,0:T(8,128)(2,1)S(1)}, u32[]{:S(2)}, u32[]{:S(2)}) async-start(bf16[8,32,2048]{2,1,0:T(8,128)(2,1)} %get-tuple-element.14), calls=%async_computation | async-start | bytes 2097152 | tf_op jit(solution)/shard_map/all_to_all | solution.py:236

commit v8 on v7

--- a/solution.py
+++ b/solution.py
@@ -81,21 +81,20 @@
     early = pltpu.make_async_copy(t_hbm.at[:, pl.ds(0, EARLY)], t_ref, t_sem)
     early.start()
     out_ref[...] = jnp.zeros_like(out_ref)
-    for copy in copies:
+    for copy in copies[:3]:
         copy.wait()
     column = to_rows(occ[...].astype(F32), O, 0).astype(I32)
-    row = c_irrep[0, place()] ^ occ[...]
-    same = column ^ row
+    same = column ^ (c_irrep[0, place()] ^ occ[...])
+    kept = [same == b_irrep[0, b] for b in range(SLABS)]
+    copies[3].wait()
     w = w_ref[...].astype(F32)
+    sends = []
     for b in range(SLABS):
-        kept = jnp.where(same == b_irrep[0, b], w[O * b : O * (b + 1)], 0.0).astype(BF16)
-        out_ref[b, :O, :O] = kept
-    sends = [
-        pltpu.make_async_copy(out_ref, out_hbm.at[pl.ds(SLABS * high, SLABS)], out_sem.at[high])
-        for high in range(2)
-    ]
-    for send in sends:
-        send.start()
+        out_ref[b, :O, :O] = jnp.where(kept[b], w[O * b : O * (b + 1)], 0.0).astype(BF16)
+        for high in range(2):
+            at = SLABS * high + b
+            sends.append(pltpu.make_async_copy(out_ref.at[b], out_hbm.at[at], out_sem.at[at]))
+            sends[-1].start()
     for send in sends:
         send.wait()
     early.wait()
@@ -212,7 +211,7 @@
         out_specs=[HBM, whole],
         scratch_shapes=[
             smem((1, 4), I32), smem((1, 512), I32), vmem((1, O), I32), vmem((COLS, O), BF16),
-            vmem((SLABS, SP, KP), BF16), dma((4,)), dma, dma((2,)),
+            vmem((SLABS, SP, KP), BF16), dma((4,)), dma, dma((2 * SLABS,)),
         ],
     )(b_row, c_row, occ, w_cycle.T, t_slab)
     w_got = lax.all_to_all(w_parts, "rep", split_axis=0, concat_axis=0, tiled=True)

time: 71 us -> 70.9 us (level)
  no operation moved by 1% of the time
where the time goes in v8:
time: 70.9 us; the launch traced here: 70.6 us
  blocking collectives  47.6 us (67%)
  starting transfers between devices  13.8 us (19%)
  Pallas kernels  6 us (8%)
  waiting for transfers between devices  3.13 us (4%)
    all_gather x1, blocking collectives, per_device(): lax.all_gather(w_own, ('idx', 'rep'), axis=0, axis_index_groups=Z_CORE_GR...  36.1 us
    all_to_all x1, blocking collectives, per_device(): lax.all_to_all(partial.reshape(2 * XS, RP, CS * NP), ('idx', 'rep'), spli...  11.6 us
    all_to_all x1, starting transfers between devices, per_device(): lax.all_to_all(w_parts, 'rep', split_axis=0, concat_axis=0, tiled=True)  10.2 us
    all_to_all x1, starting transfers between devices, per_device(): lax.all_to_all(t_parts, ('idx', 'rep'), split_axis=0, concat_axis=0, axis...  3.56 us
    all_to_all x1, waiting for transfers between devices, per_device(): lax.all_to_all(w_parts, 'rep', split_axis=0, concat_axis=0, tiled=True)  3.12 us
    pallas_call x1, Pallas kernels, per_device(): call(t_kernel, [pltpu.HBM((2 * XS, RP, ZS * KP), BF16), vmem((SLABS, ROWS...  3.08 us
    pallas_call x1, Pallas kernels, per_device(): call(head_kernel, [pltpu.HBM((2 * SLABS, SP, KP), BF16), vmem((ROWS, EARL...  1.73 us
  transfers between devices with their start and end apart: 2, of which 1 were waited for; matrix products, arithmetic and copies ran while one was open for 0% of the time, Pallas kernels for 4%

profile of v8, /device:TPU:1, one launch (start us, length us, event | category | flops | bytes accessed | tf_op | source)
XLA Modules:
  0.0 70.6 jit_solution(14217774535188922528)
XLA Ops:
  0.0 1.7 %shard_map.91 = (bf16[8,112,128]{2,1,0:T(8,128)(2,1)}, bf16[25,25600]{1,0:T(8,128)(2,1)S(1)}) custom-call(s32[1,4]{1,0:T(1,128)} %bitcast.19, s32[1,512]{1,0:T(1,128)} %bitcast.15, s32[1,100]{1,0:T(1,128)} %bitcast.17, bf16[400,100]{1,0:T(8,128)(2,1)} %bitcast.14, bf16[25,51200]{1,0:T(8,128)(2,1)} %t_hbm.3), custom_call_target="tpu_custom_call" | custom-call | flops 10000000 | bytes 1000000 | tf_op jit(solution)/shard_map/pallas_call | solution.py:206
  1.7 10.2 %all-to-all-start.1 = ((bf16[8,112,128]{2,1,0:T(8,128)(2,1)}), bf16[8,112,128]{2,1,0:T(8,128)(2,1)S(1)}, u32[]{:S(2)}, u32[]{:S(2)}) async-start(bf16[8,112,128]{2,1,0:T(8,128)(2,1)} %get-tuple-element.15), calls=%async_computation.1 | async-start | bytes 458752 | tf_op jit(solution)/shard_map/all_to_all | solution.py:217
  11.9 3.1 %shard_map.92 = (bf16[8,32,2048]{2,1,0:T(8,128)(2,1)}, f32[4,25,100]{2,1,0:T(8,128)S(1)}, f32[4,25,100]{2,1,0:T(8,128)S(1)}) custom-call(s32[1,128]{1,0:T(1,128)} %bitcast.21, s32[1,512]{1,0:T(1,128)} %bitcast.16, s32[1,100]{1,0:T(1,128)} %bitcast.18, s32[1,4]{1,0:T(1,128)} %bitcast.20, f32[1,128]{1,0:T(1,128)} %bitcast.22, f32[1,4]{1,0:T(1,128)} %bitcast.23, ...), custom_call_target="tpu_custom_call" | custom-call | flops 4000000000 | bytes 4000000 | tf_op jit(solution)/shard_map/pallas_call | solution.py:219
  15.0 3.1 %all-to-all-done.1 = bf16[8,112,128]{2,1,0:T(8,128)(2,1)S(1)} async-done(((bf16[8,112,128]{2,1,0:T(8,128)(2,1)}), bf16[8,112,128]{2,1,0:T(8,128)(2,1)S(1)}, u32[]{:S(2)}, u32[]{:S(2)}) %all-to-all-start.1) | async-done | bytes 229408 | tf_op jit(solution)/shard_map/all_to_all | solution.py:217
  18.2 3.6 %all-to-all-start = ((bf16[8,32,2048]{2,1,0:T(8,128)(2,1)}), bf16[8,32,2048]{2,1,0:T(8,128)(2,1)S(1)}, u32[]{:S(2)}, u32[]{:S(2)}) async-start(bf16[8,32,2048]{2,1,0:T(8,128)(2,1)} %get-tuple-element.14), calls=%async_computation | async-start | bytes 2097152 | tf_op jit(solution)/shard_map/all_to_all | solution.py:235
  21.8 36.1 %all-gather = bf16[3584,128]{1,0:T(8,128)(2,1)S(1)} all-gather(bf16[112,128]{1,0:T(8,128)(2,1)S(1)} %reduce_sum.9), channel_id=2, replica_groups={{0,1,8,9,16,17,24,25,32,33,40,41,48,49,56,57,64,65,72,73,80,81,88,89,96..., dimensions={0}, use_global_device_ids=true | all-gather | bytes 946176 | tf_op jit(solution)/shard_map/all_gather | solution.py:239
  57.8 0.0 all-to-all-done
  57.8 0.5 shard_map.93
  58.3 11.6 %all_to_all.15.part_ref = f32[8,32,256]{2,1,0:T(8,128)S(1)} all-to-all(f32[8,32,256]{2,1,0:T(8,128)S(1)} %bitcast.13), channel_id=1, replica_groups={{0,2,128,130,256,258,384,386},{1,3,129,131,257,259,385,387},{4,6,132,13..., dimensions={0} | all-to-all | bytes 524288 | tf_op jit(solution)/shard_map/all_to_all | solution.py:244
  69.9 0.7 %shard_map.94 = f32[25,400]{1,0:T(8,128)} custom-call(f32[4,25,100]{2,1,0:T(8,128)S(1)} %get-tuple-element.12.energy_ref, f32[4,25,100]{2,1,0:T(8,128)S(1)} %get-tuple-element.13.same_ref, f32[8,32,256]{2,1,0:T(8,128)S(1)} %all_to_all.15.part_ref), custom_call_target="tpu_custom_call" | custom-call | flops 1000000 | bytes 1000000 | tf_op jit(solution)/shard_map/pallas_call | solution.py:248
  (1 shorter events, 0.0 us)
Async XLA Ops:
  1.7 16.4 %all-to-all-start.1 = ((bf16[8,112,128]{2,1,0:T(8,128)(2,1)}), bf16[8,112,128]{2,1,0:T(8,128)(2,1)S(1)}, u32[]{:S(2)}, u32[]{:S(2)}) async-start(bf16[8,112,128]{2,1,0:T(8,128)(2,1)} %get-tuple-element.15), calls=%async_computation.1 | async-start | bytes 458752 | tf_op jit(solution)/shard_map/all_to_all | solution.py:217
  18.2 39.7 %all-to-all-start = ((bf16[8,32,2048]{2,1,0:T(8,128)(2,1)}), bf16[8,32,2048]{2,1,0:T(8,128)(2,1)S(1)}, u32[]{:S(2)}, u32[]{:S(2)}) async-start(bf16[8,32,2048]{2,1,0:T(8,128)(2,1)} %get-tuple-element.14), calls=%async_computation | async-start | bytes 2097152 | tf_op jit(solution)/shard_map/all_to_all | solution.py:235

commit v9 on v8

--- a/solution.py
+++ b/solution.py
@@ -14,6 +14,7 @@
 KP = 128
 RP = 32
 ROWS = 25
+STACK = 56
 GROUP = G * O
 CHUNK = 4 * GROUP
 CHUNKS = 16
@@ -171,18 +172,20 @@
     for c in range(CS):
         rows += [jnp.concatenate([w_ref[CS * z + c] for z in range(ZS)], axis=1), none]
     w_t = jnp.concatenate(rows, axis=0)
-    out_ref[...] = lax.dot_general(
-        t_ref[...], w_t, (((1,), (1,)), ((), ())), preferred_element_type=F32
-    )
+    got = lax.dot_general(t_ref[...], w_t, (((1,), (1,)), ((), ())), preferred_element_type=F32)
+    for to in range(2 * XS):
+        for c in range(CS):
+            out_ref[to, ROWS * c : ROWS * (c + 1), :] = got[RP * to : RP * to + ROWS, NP * c : NP * (c + 1)]
+        out_ref[to, CS * ROWS :, :] = jnp.zeros((STACK - CS * ROWS, NP), F32)
 
 
 def end_kernel(energy_ref, same_ref, part_ref, out_ref):
     for b in range(SLABS):
         low, c = divmod(b, CS)
-        lanes = slice(NP * c, NP * c + O)
-        total = part_ref[low, :ROWS, lanes]
+        rows = slice(ROWS * c, ROWS * (c + 1))
+        total = part_ref[low, rows, :O]
         for x in range(1, XS):
-            total = total + part_ref[2 * x + low, :ROWS, lanes]
+            total = total + part_ref[2 * x + low, rows, :O]
         total = jnp.where(same_ref[b] > 0.5, total, 0.0)
         out_ref[:, O * b : O * (b + 1)] = total / energy_ref[b]
 
@@ -238,11 +241,11 @@
     w_own, t_parts = lax.optimization_barrier((w_own, t_parts))
     w_z = lax.all_gather(w_own, ("idx", "rep"), axis=0, axis_index_groups=Z_CORE_GROUPS)
     partial = call(
-        mm_kernel, struct((2 * XS * RP, CS * NP), F32), 2 * 512 * 2048 * 128, 3 * 10**6, 24,
+        mm_kernel, struct((2 * XS, STACK, NP), F32), 2 * 512 * 2048 * 128, 3 * 10**6, 24,
         in_specs=[whole] * 2, out_specs=whole,
     )(t_got.reshape(-1, ZS * KP), w_z)
     ends = lax.all_to_all(
-        partial.reshape(2 * XS, RP, CS * NP), ("idx", "rep"), split_axis=0, concat_axis=0,
+        partial, ("idx", "rep"), split_axis=0, concat_axis=0,
         axis_index_groups=WORK_GROUPS, tiled=True,
     )
     return call(

time: 70.9 us -> 70.5 us (level)
  no operation moved by 1% of the time
where the time goes in v9:
time: 70.5 us; the launch traced here: 70.2 us
  blocking collectives  47.3 us (67%)
  starting transfers between devices  13.8 us (20%)
  Pallas kernels  6 us (9%)
  waiting for transfers between devices  3.13 us (4%)
    all_gather x1, blocking collectives, per_device(): lax.all_gather(w_own, ('idx', 'rep'), axis=0, axis_index_groups=Z_CORE_GR...  36.1 us
    all_to_all x1, blocking collectives, per_device(): lax.all_to_all(partial, ('idx', 'rep'), split_axis=0, concat_axis=0, axis...  11.2 us
    all_to_all x1, starting transfers between devices, per_device(): lax.all_to_all(w_parts, 'rep', split_axis=0, concat_axis=0, tiled=True)  10.2 us
    all_to_all x1, starting transfers between devices, per_device(): lax.all_to_all(t_parts, ('idx', 'rep'), split_axis=0, concat_axis=0, axis...  3.56 us
    all_to_all x1, waiting for transfers between devices, per_device(): lax.all_to_all(w_parts, 'rep', split_axis=0, concat_axis=0, tiled=True)  3.12 us
    pallas_call x1, Pallas kernels, per_device(): call(t_kernel, [pltpu.HBM((2 * XS, RP, ZS * KP), BF16), vmem((SLABS, ROWS...  3.08 us
    pallas_call x1, Pallas kernels, per_device(): call(head_kernel, [pltpu.HBM((2 * SLABS, SP, KP), BF16), vmem((ROWS, EARL...  1.73 us
  transfers between devices with their start and end apart: 2, of which 1 were waited for; matrix products, arithmetic and copies ran while one was open for 0% of the time, Pallas kernels for 4%

profile of v9, /device:TPU:1, one launch (start us, length us, event | category | flops | bytes accessed | tf_op | source)
XLA Modules:
  0.0 70.2 jit_solution(138139038559199990)
XLA Ops:
  0.0 1.7 %shard_map.91 = (bf16[8,112,128]{2,1,0:T(8,128)(2,1)}, bf16[25,25600]{1,0:T(8,128)(2,1)S(1)}) custom-call(s32[1,4]{1,0:T(1,128)} %bitcast.17, s32[1,512]{1,0:T(1,128)} %bitcast.13, s32[1,100]{1,0:T(1,128)} %bitcast.15, bf16[400,100]{1,0:T(8,128)(2,1)} %bitcast.12, bf16[25,51200]{1,0:T(8,128)(2,1)} %t_hbm.3), custom_call_target="tpu_custom_call" | custom-call | flops 10000000 | bytes 1000000 | tf_op jit(solution)/shard_map/pallas_call | solution.py:209
  1.7 10.2 %all-to-all-start.1 = ((bf16[8,112,128]{2,1,0:T(8,128)(2,1)}), bf16[8,112,128]{2,1,0:T(8,128)(2,1)S(1)}, u32[]{:S(2)}, u32[]{:S(2)}) async-start(bf16[8,112,128]{2,1,0:T(8,128)(2,1)} %get-tuple-element.15), calls=%async_computation.1 | async-start | bytes 458752 | tf_op jit(solution)/shard_map/all_to_all | solution.py:220
  11.9 3.1 %shard_map.92 = (bf16[8,32,2048]{2,1,0:T(8,128)(2,1)}, f32[4,25,100]{2,1,0:T(8,128)S(1)}, f32[4,25,100]{2,1,0:T(8,128)S(1)}) custom-call(s32[1,128]{1,0:T(1,128)} %bitcast.19, s32[1,512]{1,0:T(1,128)} %bitcast.14, s32[1,100]{1,0:T(1,128)} %bitcast.16, s32[1,4]{1,0:T(1,128)} %bitcast.18, f32[1,128]{1,0:T(1,128)} %bitcast.20, f32[1,4]{1,0:T(1,128)} %bitcast.21, ...), custom_call_target="tpu_custom_call" | custom-call | flops 4000000000 | bytes 4000000 | tf_op jit(solution)/shard_map/pallas_call | solution.py:222
  15.0 3.1 %all-to-all-done.1 = bf16[8,112,128]{2,1,0:T(8,128)(2,1)S(1)} async-done(((bf16[8,112,128]{2,1,0:T(8,128)(2,1)}), bf16[8,112,128]{2,1,0:T(8,128)(2,1)S(1)}, u32[]{:S(2)}, u32[]{:S(2)}) %all-to-all-start.1) | async-done | bytes 229408 | tf_op jit(solution)/shard_map/all_to_all | solution.py:220
  18.2 3.6 %all-to-all-start = ((bf16[8,32,2048]{2,1,0:T(8,128)(2,1)}), bf16[8,32,2048]{2,1,0:T(8,128)(2,1)S(1)}, u32[]{:S(2)}, u32[]{:S(2)}) async-start(bf16[8,32,2048]{2,1,0:T(8,128)(2,1)} %get-tuple-element.14), calls=%async_computation | async-start | bytes 2097152 | tf_op jit(solution)/shard_map/all_to_all | solution.py:238
  21.8 36.1 %all-gather = bf16[3584,128]{1,0:T(8,128)(2,1)S(1)} all-gather(bf16[112,128]{1,0:T(8,128)(2,1)S(1)} %reduce_sum.9), channel_id=2, replica_groups={{0,1,8,9,16,17,24,25,32,33,40,41,48,49,56,57,64,65,72,73,80,81,88,89,96..., dimensions={0}, use_global_device_ids=true | all-gather | bytes 946176 | tf_op jit(solution)/shard_map/all_gather | solution.py:242
  57.8 0.0 all-to-all-done
  57.8 0.5 shard_map.93
  58.3 11.2 %all_to_all.15.part_ref = f32[8,56,128]{2,1,0:T(8,128)S(1)} all-to-all(f32[8,56,128]{2,1,0:T(8,128)S(1)} %shard_map.93), channel_id=1, replica_groups={{0,2,128,130,256,258,384,386},{1,3,129,131,257,259,385,387},{4,6,132,13..., dimensions={0} | all-to-all | bytes 458752 | tf_op jit(solution)/shard_map/all_to_all | solution.py:247
  69.5 0.7 %shard_map.94 = f32[25,400]{1,0:T(8,128)} custom-call(f32[4,25,100]{2,1,0:T(8,128)S(1)} %get-tuple-element.12.energy_ref, f32[4,25,100]{2,1,0:T(8,128)S(1)} %get-tuple-element.13.same_ref, f32[8,56,128]{2,1,0:T(8,128)S(1)} %all_to_all.15.part_ref), custom_call_target="tpu_custom_call" | custom-call | flops 1000000 | bytes 1000000 | tf_op jit(solution)/shard_map/pallas_call | solution.py:251
  (1 shorter events, 0.0 us)
Async XLA Ops:
  1.7 16.4 %all-to-all-start.1 = ((bf16[8,112,128]{2,1,0:T(8,128)(2,1)}), bf16[8,112,128]{2,1,0:T(8,128)(2,1)S(1)}, u32[]{:S(2)}, u32[]{:S(2)}) async-start(bf16[8,112,128]{2,1,0:T(8,128)(2,1)} %get-tuple-element.15), calls=%async_computation.1 | async-start | bytes 458752 | tf_op jit(solution)/shard_map/all_to_all | solution.py:220
  18.2 39.7 %all-to-all-start = ((bf16[8,32,2048]{2,1,0:T(8,128)(2,1)}), bf16[8,32,2048]{2,1,0:T(8,128)(2,1)S(1)}, u32[]{:S(2)}, u32[]{:S(2)}) async-start(bf16[8,32,2048]{2,1,0:T(8,128)(2,1)} %get-tuple-element.14), calls=%async_computation | async-start | bytes 2097152 | tf_op jit(solution)/shard_map/all_to_all | solution.py:238
